TPU v7x, 512 devices: a whole 4x8x8 slice. The times are simulated.
512 devices in a mesh: ep: 128 (over y, z, core), et: 4 (over x).
Axes of the slice: x: 4, y: 8, z: 8, core: 2. Of those that a mesh axis runs over, the one named last changes fastest.
Arguments:
- activations: bfloat16 [16384, 2048], P('ep', 'et'), may hold values from -6 to 6
- cotangent: bfloat16 [16384, 2048], P('ep', 'et'), may hold values from -6 to 6
- expert_ids: int32 [16384, 4], P('ep'), may hold values from 0 to 63, all different within a row; in each aligned block of 128 rows (0 to 127, 128 to 255, ...) at most 10 rows name the same one
- route_probs: bfloat16 [16384, 4], P('ep'), may hold values from 0.049804688 to 0.5
- gate_weight: bfloat16 [128, 704, 2048], P('ep', 'et'), may hold values from -0.125 to 0.125
- up_weight: bfloat16 [128, 704, 2048], P('ep', 'et'), may hold values from -0.125 to 0.125
- down_weight: bfloat16 [128, 704, 2048], P('ep', 'et'), may hold values from -0.15625 to 0.15625
Outputs:
- input_grad: bfloat16 [16384, 2048], P('ep', 'et')
- prob_grad: float32 [16384, 4], P('ep')
- gate_grad: bfloat16 [128, 704, 2048], P('ep', 'et')
- up_grad: bfloat16 [128, 704, 2048], P('ep', 'et')
- down_grad: bfloat16 [128, 704, 2048], P('ep', 'et')
Inputs may be any that keep to these rules, and one draw needn't show every extreme that they name: `expert_ids`: each token names 4 different experts. Among the 128 tokens of one index of ep (aligned blocks of rows), no expert is named by more than 10 tokens, and in some blocks one expert is named by exactly 10.
All inputs are finite; a program needn't handle non-finite values.
Results may differ from a plain program's by a relative error of at most 0.017.
Values may be sent and summed in bfloat16 or wider, within the bound.
No kernel may reach another device: no remote copies, remote signals or barrier semaphores. Data moves between devices by JAX's collectives and lax.ppermute only.
A program may use at most 128 MiB of HBM per device.

v0:
```python
import jax
import jax.numpy as jnp
from jax import lax
from jax.sharding import PartitionSpec as P


def from_partner(value, axis, apart):
    mask = 2**apart
    pairs = [(source, source ^ mask) for source in range(lax.axis_size(axis))]
    return lax.ppermute(value, axis, pairs)


def silu_parts(pre_gate):
    sigmoid = jax.nn.sigmoid(pre_gate)
    return (pre_gate * sigmoid, sigmoid * (1.0 + pre_gate * (1.0 - sigmoid)))


def shards(activations, cotangent, expert_ids, route_probs, gate_weight, up_weight, down_weight):
    token_count, quarter = activations.shape
    top_count = expert_ids.shape[1]
    devices = lax.axis_size("ep")
    experts = devices // 2
    capacity = min(
        token_count, 2 * ((token_count * top_count * 5 // 4 + 2 * experts - 1) // (2 * experts))
    )
    half_slots = capacity // 2
    parity = lax.axis_index("ep") % 2
    flat_ids = expert_ids.reshape(-1)
    routes = flat_ids.shape[0]
    one_hot = (flat_ids[:, None] == jnp.arange(experts, dtype=jnp.int32)[None, :]).astype(jnp.int32)
    before = jnp.cumsum(one_hot, axis=0, dtype=jnp.int32) - one_hot
    position = jnp.sum(before * one_hot, axis=1, dtype=jnp.int32)
    slot_index = flat_ids * capacity + position
    slot_width = experts * capacity
    picked = (slot_index[None, :] == jnp.arange(slot_width, dtype=jnp.int32)[:, None]).astype(
        jnp.int32
    )
    filled = jnp.sum(picked, axis=1, dtype=jnp.int32)
    route_of = jnp.sum(
        picked * jnp.arange(routes, dtype=jnp.int32)[None, :], axis=1, dtype=jnp.int32
    )
    token_of = route_of // top_count
    live_bf = filled.astype(jnp.bfloat16)
    send_rows = activations[token_of] * live_bf[:, None]
    send_grads = cotangent[token_of] * live_bf[:, None]
    send_probs = route_probs.reshape(-1)[route_of] * live_bf

    def twice(block):
        shaped = block.reshape((experts, 1, capacity) + block.shape[1:])
        spread = jnp.broadcast_to(shaped, (experts, 2, capacity) + block.shape[1:])
        return spread.reshape((devices * capacity,) + block.shape[1:])

    rows, grads, probs = (
        lax.all_to_all(twice(send_rows), "ep", split_axis=0, concat_axis=0, tiled=True),
        lax.all_to_all(twice(send_grads), "ep", split_axis=0, concat_axis=0, tiled=True),
        lax.all_to_all(twice(send_probs), "ep", split_axis=0, concat_axis=0, tiled=True),
    )
    full_rows, full_grads = (
        lax.all_gather(rows, "et", axis=1, tiled=True),
        lax.all_gather(grads, "et", axis=1, tiled=True),
    )
    gate_local = gate_weight[0]
    up_local = up_weight[0]
    down_local = down_weight[0]
    unit_block = gate_local.shape[0]
    wide_local = jnp.concatenate([gate_local, up_local], axis=0)
    weight_rows = probs.astype(jnp.float32)[:, None]
    contract_last = (((1,), (1,)), ((), ()))
    contract_first = (((0,), (0,)), ((), ()))
    both_pre = lax.dot_general(
        full_rows, wide_local, contract_last, preferred_element_type=jnp.float32
    )
    pre_gate = both_pre[:, :unit_block]
    pre_up = both_pre[:, unit_block:]
    silu_value, silu_slope = silu_parts(pre_gate)
    hidden = silu_value * pre_up
    scaled_hidden = (weight_rows * hidden).astype(jnp.bfloat16)
    down_back = lax.dot_general(
        full_grads, down_local, contract_last, preferred_element_type=jnp.float32
    )
    prob_part = jnp.sum(hidden * down_back, axis=1)
    hidden_back = weight_rows * down_back
    gate_back = (hidden_back * pre_up * silu_slope).astype(jnp.bfloat16)
    up_back = (hidden_back * silu_value).astype(jnp.bfloat16)
    joint_back = jnp.concatenate([gate_back, up_back], axis=1)
    wide_grad = lax.dot_general(
        joint_back, full_rows, contract_first, preferred_element_type=jnp.float32
    ).astype(jnp.bfloat16)
    gate_grad = wide_grad[:unit_block][None]
    up_grad = wide_grad[unit_block:][None]
    down_grad = lax.dot_general(
        scaled_hidden, full_grads, contract_first, preferred_element_type=jnp.float32
    ).astype(jnp.bfloat16)[None]
    block_part = jnp.dot(joint_back, wide_local, preferred_element_type=jnp.float32).astype(
        jnp.bfloat16
    )
    block_halves = block_part.reshape(devices, 2, half_slots, block_part.shape[1])
    kept_part = lax.dynamic_index_in_dim(block_halves, parity, 1, keepdims=False).reshape(
        devices * half_slots, block_part.shape[1]
    )
    given_part = lax.dynamic_index_in_dim(block_halves, 1 - parity, 1, keepdims=False).reshape(
        devices * half_slots, block_part.shape[1]
    )
    got_part = from_partner(given_part, "ep", 0)
    pair_part = (kept_part.astype(jnp.float32) + got_part.astype(jnp.float32)).astype(jnp.bfloat16)
    pair_terms = pair_part.astype(jnp.float32).reshape(devices, half_slots, pair_part.shape[1])
    route_grad = lax.psum_scatter(
        pair_terms.astype(jnp.bfloat16), "et", scatter_dimension=2, tiled=True
    ).astype(jnp.float32)
    prob_sums = lax.psum(prob_part.reshape(devices, capacity), "et")
    back_grad, back_probs = (
        lax.all_to_all(
            route_grad.astype(jnp.bfloat16), "ep", split_axis=0, concat_axis=0, tiled=True
        ).astype(route_grad.dtype),
        lax.all_to_all(
            prob_sums.astype(jnp.bfloat16), "ep", split_axis=0, concat_axis=0, tiled=True
        ).astype(prob_sums.dtype),
    )
    back_grad = back_grad.reshape(slot_width, quarter)
    back_probs = jnp.sum(back_probs.reshape(experts, 2, capacity), axis=1).reshape(slot_width)
    per_route = back_grad[slot_index].reshape(token_count, top_count, quarter)
    input_grad = jnp.sum(per_route, axis=1).astype(jnp.bfloat16)
    prob_grad = back_probs[slot_index].reshape(token_count, top_count)
    return (input_grad, prob_grad, gate_grad, up_grad, down_grad)


def solution(mesh):
    placed = (
        P("ep", "et"),
        P("ep", "et"),
        P("ep", None),
        P("ep", None),
        P("ep", "et", None),
        P("ep", "et", None),
        P("ep", "et", None),
    )
    return jax.shard_map(
        shards,
        mesh=mesh,
        in_specs=placed,
        out_specs=(
            P("ep", "et"),
            P("ep", None),
            P("ep", "et", None),
            P("ep", "et", None),
            P("ep", "et", None),
        ),
        check_vma=False,
    )
```

profile of v0, /device:TPU:1, one launch (start us, length us, event | category | flops | bytes accessed | tf_op | source)
XLA Modules:
  0.0 372.0 jit_solution(8194879856939189021)
XLA Ops:
  10.6 2.8 gather_fusion.2
  13.6 3.3 gather_fusion.1
  19.7 70.4 %all_to_all.47 = bf16[128,10,512]{2,1,0:T(8,128)(2,1)S(1)} all-to-all(bf16[128,10,512]{2,1,0:T(8,128)(2,1)S(1)} %bitcast.45), channel_id=1, replica_groups=mesh['ep'=128,'et'=4] {'ep'}, dimensions={0} | all-to-all | bytes 2621440 | tf_op jit(solution)/shard_map/all_to_all | solution.py:54
  90.0 1.3 all_to_all.38
  91.4 1.5 broadcast_in_dim.13
  92.9 59.7 %all_to_all.48 = bf16[128,10,512]{2,1,0:T(8,128)(2,1)S(1)} all-to-all(bf16[128,10,512]{2,1,0:T(8,128)(2,1)S(1)} %bitcast.46), channel_id=1, replica_groups=mesh['ep'=128,'et'=4] {'ep'}, dimensions={0} | all-to-all | bytes 2621440 | tf_op jit(solution)/shard_map/all_to_all | solution.py:55
  152.7 1.3 all_to_all.35
  154.3 4.3 %gather_fusion = bf16[640]{0:T(1024)(128)(2,1)S(1)} fusion(bf16[512]{0:T(512)(128)(2,1)S(1)} %reshape.235, s32[1024]{0:T(1024)S(1)} %get-tuple-element.39), kind=kCustom, calls=%fused_computation | custom fusion | bytes 5120 | tf_op jit(solution)/shard_map/gather | solution.py:46
  159.5 7.8 %all-to-all-start = ((bf16[128,10,1]{1,2,0:T(2,128)(2,1)}), bf16[128,10,1]{1,2,0:T(2,128)(2,1)S(1)}, u32[]{:S(2)}, u32[]{:S(2)}) async-start(bf16[128,10,1]{1,2,0:T(2,128)(2,1)} %copy.37), calls=%async_computation | async-start | bytes 131072 | tf_op jit(solution)/shard_map/all_to_all | solution.py:56
  167.5 11.2 %all-to-all-done = bf16[128,10,1]{1,2,0:T(2,128)(2,1)S(1)} async-done(((bf16[128,10,1]{1,2,0:T(2,128)(2,1)}), bf16[128,10,1]{1,2,0:T(2,128)(2,1)S(1)}, u32[]{:S(2)}, u32[]{:S(2)}) %all-to-all-start) | async-done | bytes 2592 | tf_op jit(solution)/shard_map/all_to_all | solution.py:56
  179.1 5.9 %fusion.1 = f32[1280,352]{0,1:T(8,128)} fusion(bf16[1280,2048]{1,0:T(8,128)(2,1)} %all-gather.5.cloned.1.call-done, bf16[176,2048]{1,0:T(8,128)(2,1)S(1)} %bitcast.54, bf16[176,2048]{1,0:T(8,128)(2,1)S(1)} %bitcast.56), kind=kOutput, calls=%fused_computation.15 | convolution fusion | flops 1848377344 | bytes 8486912 | tf_op jit(solution)/shard_map/dot_general | solution.py:70
  185.0 28.7 %all-gather.3.cloned.1.call-done = bf16[1280,2048]{1,0:T(8,128)(2,1)} async-done(((bf16[1280,512]{1,0:T(8,128)(2,1)}), bf16[1280,2048]{1,0:T(8,128)(2,1)}) %all-gather.3.cloned.1.call-update) | async-done | bytes 5242896 | tf_op jit(solution)/shard_map/all_gather | solution.py:60
  213.7 5.1 %multiply_convert_fusion.2 = (bf16[1280,176]{0,1:T(8,128)(2,1)S(1)}, bf16[1280,176]{0,1:T(8,128)(2,1)S(1)}, f32[1280]{0:T(1024)S(1)}) fusion(f32[1280,352]{0,1:T(8,128)} %fusion.1, f32[1280]{0:T(1024)S(1)} %reshape.246, bf16[1280,2048]{1,0:T(8,128)(2,1)} %all-gather.3.cloned.1.call-done, bf16[1,176,2048]{2,1,0:T(8,128)(2,1)S(1)} %copy-done), kind=kOutput, calls=%fused_computation.20 | convolution fusion | flops 926575360 | bytes 8677376 | tf_op jit(solution)/shard_map/dot_general | solution.py:78
  218.8 4.7 %convolution_convert_fusion = bf16[1280,2048]{1,0:T(8,128)(2,1)} fusion(bf16[176,2048]{1,0:T(8,128)(2,1)S(1)} %bitcast.55, bf16[176,2048]{1,0:T(8,128)(2,1)S(1)} %bitcast.57, bf16[1280,176]{0,1:T(8,128)(2,1)S(1)} %get-tuple-element.32, bf16[1280,176]{0,1:T(8,128)(2,1)S(1)} %get-tuple-element.31), kind=kOutput, calls=%fused_computation.5 | convolution fusion | flops 1852801024 | bytes 7585792 | tf_op jit(solution)/shard_map/dot_general | solution.py:94
  223.5 9.7 %reshape.238 = bf16[128,2,5,2048]{3,2,1,0:T(8,128)(2,1)} reshape(bf16[1280,2048]{1,0:T(8,128)(2,1)} %convolution_convert_fusion) | data formatting | bytes 10485760 | tf_op jit(solution)/shard_map/reshape | solution.py:97
  233.2 10.0 %constant_dynamic-slice_fusion = (bf16[128,1,5,2048]{3,2,1,0:T(8,128)(2,1)}, f32[128,1,5,2048]{3,2,1,0:T(8,128)}) fusion(bf16[128,2,5,2048]{3,2,1,0:T(8,128)(2,1)} %reshape.238, s32[]{:T(128)S(6)} %select_n.63, s32[]{:T(128)S(6)} %select_n.62), kind=kLoop, calls=%fused_computation.56 | loop fusion | flops 1310720 | bytes 13107208 | tf_op jit(solution)/shard_map/jit(dynamic_index_in_dim)/dynamic_slice | solution.py:101
  243.2 4.2 %reshape.239 = bf16[640,2048]{1,0:T(8,128)(2,1)S(1)} reshape(bf16[128,1,5,2048]{3,2,1,0:T(8,128)(2,1)} %get-tuple-element.29) | data formatting | bytes 5242880 | tf_op jit(solution)/shard_map/reshape | solution.py:101
  247.4 2.6 collective-permute-start
  250.0 7.5 %reshape.247 = f32[640,2048]{1,0:T(8,128)} reshape(f32[128,1,5,2048]{3,2,1,0:T(8,128)} %get-tuple-element.30) | data formatting | bytes 10485760 | tf_op jit(solution)/shard_map/convert_element_type | solution.py:105
  257.5 4.2 %add_convert_fusion = bf16[640,2048]{1,0:T(8,128)(2,1)S(1)} fusion(f32[640,2048]{1,0:T(8,128)} %reshape.247, bf16[640,2048]{1,0:T(8,128)(2,1)} %collective-permute-done), kind=kLoop, calls=%fused_computation.6 | loop fusion | flops 3932160 | bytes 10485760 | tf_op jit(solution)/shard_map/convert_element_type | solution.py:105
  261.7 2.9 convert_element_type.103
  265.6 12.1 %psum.7 = bf16[128,10]{1,0:T(8,128)(2,1)S(1)} all-reduce(f32[128,10]{1,0:T(8,128)S(1)} %reshape.243), channel_id=1, replica_groups=mesh['ep'=128,'et'=4] {'et'}, use_global_device_ids=true, to_apply=%region_8.9 | all-reduce | flops 1280 | bytes 7680 | tf_op jit(solution)/shard_map/psum | solution.py:110
  278.4 17.6 %all-to-all-start.4 = ((bf16[128,1,10]{2,1,0:T(2,128)(2,1)}), bf16[128,1,10]{2,1,0:T(2,128)(2,1)S(1)}, u32[]{:S(2)}, u32[]{:S(2)}) async-start(bf16[128,1,10]{2,1,0:T(2,128)(2,1)} %copy.39), calls=%async_computation.5 | async-start | bytes 131072 | tf_op jit(solution)/shard_map/all_to_all | solution.py:115
  296.1 11.4 %all-to-all-done.4 = bf16[128,1,10]{2,1,0:T(2,128)(2,1)S(1)} async-done(((bf16[128,1,10]{2,1,0:T(2,128)(2,1)}), bf16[128,1,10]{2,1,0:T(2,128)(2,1)S(1)}, u32[]{:S(2)}, u32[]{:S(2)}) %all-to-all-start.4) | async-done | bytes 2592 | tf_op jit(solution)/shard_map/all_to_all | solution.py:115
  307.5 9.5 %reduce-scatter.2.cloned.1.call-done = bf16[128,5,512]{2,1,0:T(8,128)(2,1)} async-done(((bf16[128,5,2048]{2,1,0:T(8,128)(2,1)}), bf16[128,5,512]{2,1,0:T(8,128)(2,1)}) %reduce-scatter.2.cloned.1.call-update) | async-done | bytes 655376 | tf_op jit(solution)/shard_map/reduce_scatter | solution.py:107
  317.0 14.6 %all-to-all-start.3 = ((bf16[128,5,512]{2,1,0:T(8,128)(2,1)}), bf16[128,5,512]{2,1,0:T(8,128)(2,1)S(1)}, u32[]{:S(2)}, u32[]{:S(2)}) async-start(bf16[128,5,512]{2,1,0:T(8,128)(2,1)} %reduce-scatter.2.cloned.1.call-done), calls=%async_computation.4 | async-start | bytes 2097152 | tf_op jit(solution)/shard_map/all_to_all | solution.py:112
  331.6 4.8 %convolution_convert_fusion.1 = bf16[352,2048]{1,0:T(8,128)(2,1)S(1)} fusion(bf16[1280,2048]{1,0:T(8,128)(2,1)} %all-gather.5.cloned.1.call-done, bf16[1280,176]{0,1:T(8,128)(2,1)} %copy-done.11, bf16[1280,176]{0,1:T(8,128)(2,1)S(1)} %copy-done.10), kind=kOutput, calls=%fused_computation.8 | convolution fusion | flops 1848016896 | bytes 7585792 | tf_op jit(solution)/shard_map/dot_general | solution.py:86
  338.4 2.1 fusion
  340.8 2.3 gather_fusion.4
  343.9 18.1 %all-to-all-done.3 = bf16[128,5,512]{2,1,0:T(8,128)(2,1)S(1)} async-done(((bf16[128,5,512]{2,1,0:T(8,128)(2,1)}), bf16[128,5,512]{2,1,0:T(8,128)(2,1)S(1)}, u32[]{:S(2)}, u32[]{:S(2)}) %all-to-all-start.3) | async-done | bytes 655392 | tf_op jit(solution)/shard_map/all_to_all | solution.py:112
  362.3 1.6 gather_fusion.3
  364.2 1.3 reduce_sum.63
  (79 shorter events, 13.4 us)
Async XLA Ops:
  7.2 206.5 %copy-start = (bf16[1,176,2048]{2,1,0:T(8,128)(2,1)S(1)}, bf16[1,176,2048]{2,1,0:T(8,128)(2,1)}, u32[]{:S(2)}) copy-start(bf16[1,176,2048]{2,1,0:T(8,128)(2,1)} %param.13) | copy-start | bytes 2162692
  7.2 3.4 copy-start.2
  7.2 171.9 %all-gather.5.cloned.1.call-start = ((), (), s32[]{:S(2)}) async-start(), calls=%async_computation.7 | async-start | bytes 6553600 | tf_op jit(solution)/shard_map/all_gather | solution.py:59
  10.6 3.0 copy-start.3
  91.4 122.3 %all-gather.3.cloned.1.call-start = ((), (), s32[]{:S(2)}) async-start(), calls=%async_computation.6 | async-start | bytes 6553600 | tf_op jit(solution)/shard_map/all_gather | solution.py:60
  152.7 1.3 copy-start.5
  154.0 25.1 %copy-start.6 = (bf16[1,176,2048]{2,1,0:T(8,128)(2,1)S(1)}, bf16[1,176,2048]{2,1,0:T(8,128)(2,1)}, u32[]{:S(2)}) copy-start(bf16[1,176,2048]{2,1,0:T(8,128)(2,1)} %param.12) | copy-start | bytes 2162692
  154.0 25.1 %copy-start.7 = (bf16[1,176,2048]{2,1,0:T(8,128)(2,1)S(1)}, bf16[1,176,2048]{2,1,0:T(8,128)(2,1)}, u32[]{:S(2)}) copy-start(bf16[1,176,2048]{2,1,0:T(8,128)(2,1)} %param.11) | copy-start | bytes 2162692
  159.5 19.2 %all-to-all-start = ((bf16[128,10,1]{1,2,0:T(2,128)(2,1)}), bf16[128,10,1]{1,2,0:T(2,128)(2,1)S(1)}, u32[]{:S(2)}, u32[]{:S(2)}) async-start(bf16[128,10,1]{1,2,0:T(2,128)(2,1)} %copy.37), calls=%async_computation | async-start | bytes 131072 | tf_op jit(solution)/shard_map/all_to_all | solution.py:56
  167.3 149.7 %reduce-scatter.2.cloned.1.call-start = ((), (), s32[]{:S(2)}) async-start(), calls=%async_computation.8 | async-start | bytes 5242880 | tf_op jit(solution)/shard_map/reduce_scatter | solution.py:107
  218.8 4.7 %copy-start.9 = (bf16[1280,176]{0,1:T(8,128)(2,1)}, bf16[1280,176]{0,1:T(8,128)(2,1)S(1)}, u32[]{:S(2)}) copy-start(bf16[1280,176]{0,1:T(8,128)(2,1)S(1)} %get-tuple-element.31) | copy-start | bytes 1351684
  218.8 4.7 %copy-start.11 = (bf16[1280,176]{0,1:T(8,128)(2,1)}, bf16[1280,176]{0,1:T(8,128)(2,1)S(1)}, u32[]{:S(2)}) copy-start(bf16[1280,176]{0,1:T(8,128)(2,1)S(1)} %get-tuple-element.32) | copy-start | bytes 1351684
  247.4 10.1 %collective-permute-start = (bf16[640,2048]{1,0:T(8,128)(2,1)S(1)}, bf16[640,2048]{1,0:T(8,128)(2,1)}, u32[]{:S(2)}, u32[]{:S(2)}) collective-permute-start(bf16[640,2048]{1,0:T(8,128)(2,1)S(1)} %reshape.239), channel_id=1, source_target_pairs={{0,4},{4,0},{8,12},{12,8},{16,20},{20,16},{24,28},{28,24},{32,36},... | collective-permute-start | bytes 7864328 | tf_op jit(solution)/shard_map/ppermute | solution.py:10
  264.6 0.7 copy-start.4
  264.6 67.0 %copy-start.10 = (bf16[1280,176]{0,1:T(8,128)(2,1)S(1)}, bf16[1280,176]{0,1:T(8,128)(2,1)}, u32[]{:S(2)}) copy-start(bf16[1280,176]{0,1:T(8,128)(2,1)} %copy-done.9) | copy-start | bytes 1351684
  278.4 29.1 %all-to-all-start.4 = ((bf16[128,1,10]{2,1,0:T(2,128)(2,1)}), bf16[128,1,10]{2,1,0:T(2,128)(2,1)S(1)}, u32[]{:S(2)}, u32[]{:S(2)}) async-start(bf16[128,1,10]{2,1,0:T(2,128)(2,1)} %copy.39), calls=%async_computation.5 | async-start | bytes 131072 | tf_op jit(solution)/shard_map/all_to_all | solution.py:115
  317.0 20.6 %slice-start = ((s8[5242880]{0:T(1024)(128)(4,1)}), s8[1048576]{0:T(1024)(128)(4,1)S(1)}, s32[]{:S(2)}) async-start(s8[5242880]{0:T(1024)(128)(4,1)} %bitcast.52), calls=%async_computation.9 | async-start | bytes 2097152
  317.0 45.0 %all-to-all-start.3 = ((bf16[128,5,512]{2,1,0:T(8,128)(2,1)}), bf16[128,5,512]{2,1,0:T(8,128)(2,1)S(1)}, u32[]{:S(2)}, u32[]{:S(2)}) async-start(bf16[128,5,512]{2,1,0:T(8,128)(2,1)} %reduce-scatter.2.cloned.1.call-done), calls=%async_computation.4 | async-start | bytes 2097152 | tf_op jit(solution)/shard_map/all_to_all | solution.py:112
  331.6 6.0 %slice-start.1 = ((s8[5242880]{0:T(1024)(128)(4,1)}), s8[4194304]{0:T(1024)(128)(4,1)S(1)}, s32[]{:S(2)}) async-start(s8[5242880]{0:T(1024)(128)(4,1)} %bitcast.52), calls=%async_computation.10 | async-start | bytes 8388608
  336.4 2.0 copy-start.8
  362.2 3.3 copy-start.1
Sparse Core Ops, SparseCore 0:
  91.5 57.1 all-gather.4
  154.1 59.4 all-gather.2
  264.7 52.1 reduce-scatter.1
where the time goes:
time: 373 us; the launch traced here: 372 us
  blocking collectives  142 us (38%)
  waiting for transfers between devices  79 us (21%)
  local copies, waits for them, and re-layouts  52.3 us (14%)
  starting transfers between devices  42.9 us (12%)
  matrix products  22.6 us (6%)
  other arithmetic  18.9 us (5%)
  between operations  14.2 us (4%)
    all_to_all x1, blocking collectives, shards(): lax.all_to_all(twice(send_rows), 'ep', split_axis=0, concat_axis=0, tiled...  70.4 us
    all_to_all x1, blocking collectives, shards(): lax.all_to_all(twice(send_grads), 'ep', split_axis=0, concat_axis=0, tile...  59.7 us
    all_gather x1, waiting for transfers between devices, shards(): lax.all_gather(grads, 'et', axis=1, tiled=True)  28.7 us
    all_to_all x1, waiting for transfers between devices, shards(): lax.all_to_all(route_grad.astype(jnp.bfloat16), 'ep', split_axis=0, conca...  18.1 us
    all_to_all x1, starting transfers between devices, shards(): lax.all_to_all(prob_sums.astype(jnp.bfloat16), 'ep', split_axis=0, concat...  17.6 us
    all_to_all x1, starting transfers between devices, shards(): lax.all_to_all(route_grad.astype(jnp.bfloat16), 'ep', split_axis=0, conca...  14.6 us
    psum x1, blocking collectives, shards(): prob_sums = lax.psum(prob_part.reshape(devices, capacity), 'et')  12.1 us
    all_to_all x1, waiting for transfers between devices, shards(): lax.all_to_all(prob_sums.astype(jnp.bfloat16), 'ep', split_axis=0, concat...  11.4 us
  transfers between devices with their start and end apart: 7, of which 5 were waited for; matrix products, arithmetic and copies ran while one was open for 9% of the time, Pallas kernels for 0%

commit v1 on v0

v1 whole, which is shorter than its diff:
```python
import jax
import jax.numpy as jnp
from jax import lax
from jax.sharding import PartitionSpec as P

CAPACITY = 10
HEAD = 8
REST = CAPACITY - HEAD


def silu_parts(pre_gate):
    sigmoid = jax.nn.sigmoid(pre_gate)
    return (pre_gate * sigmoid, sigmoid * (1.0 + pre_gate * (1.0 - sigmoid)))


def dot_f32(left, right, left_dim, right_dim):
    return lax.dot_general(
        left, right, (((left_dim,), (right_dim,)), ((), ())), preferred_element_type=jnp.float32
    )


def same_core_groups(devices):
    return [list(range(core, devices, 2)) for core in range(2)]


def exchange_chips(block):
    return lax.all_to_all(
        block,
        "ep",
        split_axis=0,
        concat_axis=0,
        axis_index_groups=same_core_groups(lax.axis_size("ep")),
        tiled=True,
    )


def other_core(value):
    pairs = [(source, source ^ 1) for source in range(lax.axis_size("ep"))]
    return lax.ppermute(value, "ep", pairs)


def exchange_x(block):
    return lax.all_to_all(block, "et", split_axis=0, concat_axis=0, tiled=True)


def gather_x(block):
    count = lax.axis_size("et")
    copies = jnp.broadcast_to(block[None], (count,) + block.shape)
    parts = exchange_x(copies)
    return jnp.concatenate([parts[index] for index in range(count)], axis=1)


def two_halves(value):
    high = value.astype(jnp.bfloat16)
    low = (value - high.astype(jnp.float32)).astype(jnp.bfloat16)
    return high, low


def expand(values, experts, width):
    columns = jnp.arange(experts * width, dtype=jnp.int32) // width
    spread = (columns[None, :] == jnp.arange(experts, dtype=jnp.int32)[:, None]).astype(jnp.bfloat16)
    return dot_f32(values.astype(jnp.bfloat16), spread, 1, 0)


def shards(activations, cotangent, expert_ids, route_probs, gate_weight, up_weight, down_weight):
    tokens, quarter = activations.shape
    top_count = expert_ids.shape[1]
    experts = lax.axis_size("ep") // 2
    x_count = lax.axis_size("et")
    bf16 = jnp.bfloat16
    f32 = jnp.float32

    own_weights = jnp.concatenate([gate_weight[0], up_weight[0], down_weight[0]], axis=0)
    other_weights = other_core(own_weights)

    hits = expert_ids[:, :, None] == jnp.arange(experts, dtype=jnp.int32)[None, None, :]
    hit = jnp.sum(hits.astype(f32), axis=1)
    weight = jnp.sum(jnp.where(hits, route_probs.astype(f32)[:, :, None], 0.0), axis=1)
    row = jnp.arange(tokens, dtype=jnp.int32)
    earlier = (row[None, :] < row[:, None]).astype(bf16)
    rank = dot_f32(earlier, hit.astype(bf16), 1, 0)
    code = jnp.where(hit > 0.0, rank, 255.0)

    def selection(width, first):
        place = (jnp.arange(experts * width, dtype=jnp.int32) % width + first).astype(f32)
        return (expand(code, experts, width) == place[None, :]).astype(bf16)

    head_pick = selection(HEAD, 0)
    rest_pick = selection(REST, HEAD)
    head_weighted = head_pick * expand(weight, experts, HEAD).astype(bf16)
    rest_weighted = rest_pick * expand(weight, experts, REST).astype(bf16)
    head_send = jnp.concatenate(
        [
            dot_f32(head_pick, activations, 0, 0).astype(bf16),
            dot_f32(head_weighted, cotangent, 0, 0).astype(bf16),
        ],
        axis=1,
    )
    rest_send = jnp.concatenate(
        [
            dot_f32(rest_pick, activations, 0, 0).astype(bf16),
            dot_f32(rest_weighted, cotangent, 0, 0).astype(bf16),
        ],
        axis=1,
    )

    def fold_rest(block):
        folds = HEAD // REST
        lanes = block.shape[1] // folds
        shaped = block.reshape(experts, REST, folds, lanes).transpose(0, 2, 1, 3)
        return shaped.reshape(experts * HEAD, lanes)

    def unfold_rest(block):
        folds = HEAD // REST
        lanes = block.shape[1]
        shaped = block.reshape(experts, folds, REST, lanes).transpose(0, 2, 1, 3)
        return shaped.reshape(experts * REST, folds * lanes)

    send = jnp.concatenate([head_send, fold_rest(rest_send)], axis=1)
    got = exchange_chips(send.reshape(experts, HEAD, send.shape[1])).reshape(send.shape)
    got_rest = unfold_rest(got[:, 2 * quarter :])
    rows = jnp.concatenate([got[:, :quarter], got_rest[:, :quarter]], axis=0)
    grads = jnp.concatenate([got[:, quarter : 2 * quarter], got_rest[:, quarter:]], axis=0)
    full_rows = gather_x(rows)
    full_grads = gather_x(grads)
    slots = full_rows.shape[0]

    units = gate_weight.shape[1]
    wide = jnp.concatenate([own_weights[: 2 * units], other_weights[: 2 * units]], axis=0)
    down = jnp.concatenate([own_weights[2 * units :], other_weights[2 * units :]], axis=0)
    both_pre = dot_f32(full_rows, wide, 1, 1).reshape(slots, 2, 2, units)
    pre_gate = both_pre[:, :, 0].reshape(slots, 2 * units)
    pre_up = both_pre[:, :, 1].reshape(slots, 2 * units)
    silu_value, silu_slope = silu_parts(pre_gate)
    hidden = silu_value * pre_up
    down_back = dot_f32(full_grads, down, 1, 1)
    gate_back = (down_back * pre_up * silu_slope).astype(bf16)
    up_back = (down_back * silu_value).astype(bf16)
    prob_part = jnp.sum(hidden * down_back, axis=1)
    joint_back = jnp.concatenate(
        [gate_back[:, :units], up_back[:, :units], gate_back[:, units:], up_back[:, units:]], axis=1
    )
    block_part = dot_f32(joint_back, wide, 1, 0).astype(bf16)

    high, low = two_halves(prob_part)
    prob_rows = jnp.concatenate([high, low]).reshape(-1)
    prob_rows = jnp.pad(prob_rows, (0, 8 * quarter - prob_rows.shape[0])).reshape(8, quarter)
    parts = jnp.stack(
        [
            jnp.concatenate([block_part[:, i * quarter : (i + 1) * quarter], prob_rows], axis=0)
            for i in range(x_count)
        ]
    )
    summed = jnp.sum(exchange_x(parts).astype(f32), axis=0)
    route_grad = summed[:slots].astype(bf16)
    prob_flat = summed[slots:].reshape(-1)
    prob_sums = prob_flat[:slots] + prob_flat[slots : 2 * slots]
    prob_sums = jnp.concatenate(
        [
            prob_sums[: experts * HEAD].reshape(experts, HEAD),
            prob_sums[experts * HEAD :].reshape(experts, REST),
        ],
        axis=1,
    )
    sum_high, sum_low = two_halves(prob_sums)
    prob_tile = jnp.pad(
        jnp.stack([sum_high, sum_low], axis=1), ((0, 0), (0, HEAD - 2), (0, 128 - CAPACITY))
    ).reshape(experts * HEAD, 128)
    give = jnp.concatenate(
        [route_grad[: experts * HEAD], fold_rest(route_grad[experts * HEAD :]), prob_tile], axis=1
    )
    back = exchange_chips(give.reshape(experts, HEAD, give.shape[1])).reshape(give.shape)
    back_rest = unfold_rest(back[:, quarter : quarter + quarter * REST // HEAD])
    input_grad = (
        dot_f32(head_pick, back[:, :quarter], 1, 0) + dot_f32(rest_pick, back_rest, 1, 0)
    ).astype(bf16)
    back_probs = back[:, -128:].reshape(experts, HEAD, 128)[:, :2, :CAPACITY].astype(f32)
    back_probs = jnp.sum(back_probs, axis=1)
    by_expert = jnp.zeros((tokens, experts), f32)
    for place in range(CAPACITY):
        by_expert += jnp.where(code == place, back_probs[:, place][None, :], 0.0)
    prob_grad = jnp.sum(jnp.where(hits, by_expert[:, None, :], 0.0), axis=2)
    prob_grad = prob_grad / route_probs.astype(f32)

    wide_part = dot_f32(joint_back, full_rows, 0, 0)
    down_part = dot_f32(hidden.astype(bf16), full_grads, 0, 0)
    given = jnp.concatenate([wide_part[2 * units :], down_part[units:]], axis=0).astype(bf16)
    taken = other_core(given).astype(f32)
    gate_grad = (wide_part[:units] + taken[:units]).astype(bf16)[None]
    up_grad = (wide_part[units : 2 * units] + taken[units : 2 * units]).astype(bf16)[None]
    down_grad = (down_part[:units] + taken[2 * units :]).astype(bf16)[None]
    return (input_grad, prob_grad, gate_grad, up_grad, down_grad)


def solution(mesh):
    placed = (
        P("ep", "et"),
        P("ep", "et"),
        P("ep", None),
        P("ep", None),
        P("ep", "et", None),
        P("ep", "et", None),
        P("ep", "et", None),
    )
    return jax.shard_map(
        shards,
        mesh=mesh,
        in_specs=placed,
        out_specs=(
            P("ep", "et"),
            P("ep", None),
            P("ep", "et", None),
            P("ep", "et", None),
            P("ep", "et", None),
        ),
        check_vma=False,
    )
```

time: 373 us -> 219 us (0.59)
  the two profiles are of different devices: /device:TPU:1 before, /device:TPU:16 now
where the time goes in v1:
time: 219 us; the launch traced here: 218 us
  waiting for transfers between devices  73.6 us (34%)
  blocking collectives  52 us (24%)
  starting transfers between devices  31.2 us (14%)
  local copies, waits for them, and re-layouts  20.8 us (9%)
  other arithmetic  20.1 us (9%)
  matrix products  18.6 us (8%)
    all_to_all x3, waiting for transfers between devices, exchange_x(): return lax.all_to_all(block, 'et', split_axis=0, concat_axis=0, tiled=True)  57.5 us
    all_to_all x1, blocking collectives, exchange_chips(): lax.all_to_all(block, 'ep', split_axis=0, concat_axis=0, axis_index_group...  52 us
    dot_general x14, matrix products, dot_f32(): lax.dot_general(left, right, (((left_dim,), (right_dim,)), ((), ())), pre...  18.6 us
    all_to_all x1, waiting for transfers between devices, exchange_chips(): lax.all_to_all(block, 'ep', split_axis=0, concat_axis=0, axis_index_group...  16.1 us
    all_to_all x1, starting transfers between devices, exchange_chips(): lax.all_to_all(block, 'ep', split_axis=0, concat_axis=0, axis_index_group...  14.4 us
    all_to_all x3, starting transfers between devices, exchange_x(): return lax.all_to_all(block, 'et', split_axis=0, concat_axis=0, tiled=True)  13 us
    unnamed x84, local copies, waits for them, and re-layouts  6.2 us
  transfers between devices with their start and end apart: 6, of which 4 were waited for; matrix products, arithmetic and copies ran while one was open for 14% of the time, Pallas kernels for 0%

profile of v1, /device:TPU:16, one launch (start us, length us, event | category | flops | bytes accessed | tf_op | source)
XLA Modules:
  0.0 217.9 jit_solution(17355661838282157199)
XLA Ops:
  2.7 1.1 convolution_convert_fusion.4
  4.7 1.2 fusion.8
  6.6 52.0 %all_to_all.25 = bf16[64,8,1280]{2,1,0:T(8,128)(2,1)S(1)} all-to-all(bf16[64,8,1280]{2,1,0:T(8,128)(2,1)S(1)} %pad_maximum_fusion.10), channel_id=1, replica_groups={{0,8,16,24,32,40,48,56,64,72,80,88,96,104,112,120,128,136,144,152,160,1..., dimensions={0} | all-to-all | bytes 2621440 | tf_op jit(solution)/shard_map/all_to_all | solution.py:27
  59.9 1.7 broadcast_in_dim.151
  61.6 4.4 %all-to-all-start.2 = ((bf16[4,640,512]{2,1,0:T(8,128)(2,1)}), bf16[4,640,512]{2,1,0:T(8,128)(2,1)S(1)}, u32[]{:S(2)}, u32[]{:S(2)}) async-start(bf16[4,640,512]{2,1,0:T(8,128)(2,1)} %broadcast_in_dim.151), calls=%async_computation.2 | async-start | bytes 5242880 | tf_op jit(solution)/shard_map/all_to_all | solution.py:43
  66.0 2.9 %pad_maximum_fusion.4 = bf16[528,2048]{1,0:T(8,128)(2,1)} fusion(bf16[176,2048]{1,0:T(8,128)(2,1)S(1)} %bitcast.121, bf16[176,2048]{1,0:T(8,128)(2,1)} %bitcast.123, bf16[176,2048]{1,0:T(8,128)(2,1)} %bitcast.126), kind=kLoop, calls=%fused_computation.7 | loop fusion | flops 6488064 | bytes 4325376 | tf_op jit(solution)/shard_map/concatenate | solution.py:73
  68.9 1.9 collective-permute-start
  70.9 24.3 %all-to-all-done.2 = bf16[4,640,512]{2,1,0:T(8,128)(2,1)S(1)} async-done(((bf16[4,640,512]{2,1,0:T(8,128)(2,1)}), bf16[4,640,512]{2,1,0:T(8,128)(2,1)S(1)}, u32[]{:S(2)}, u32[]{:S(2)}) %all-to-all-start.2) | async-done | bytes 2621472 | tf_op jit(solution)/shard_map/all_to_all | solution.py:43
  95.2 1.7 broadcast_in_dim.150
  96.9 4.6 %all-to-all-start.1 = ((bf16[4,640,512]{2,1,0:T(8,128)(2,1)}), bf16[4,640,512]{2,1,0:T(8,128)(2,1)}, u32[]{:S(2)}, u32[]{:S(2)}) async-start(bf16[4,640,512]{2,1,0:T(8,128)(2,1)} %broadcast_in_dim.150), calls=%async_computation.1 | async-start | bytes 5242880 | tf_op jit(solution)/shard_map/all_to_all | solution.py:43
  101.5 2.0 slice.249
  103.6 1.5 slice.256
  107.5 2.4 %fusion.10 = f32[640,704]{0,1:T(8,128)S(1)} fusion(bf16[352,2048]{1,0:T(8,128)(2,1)S(1)} %slice.256, bf16[176,2048]{1,0:T(8,128)(2,1)S(1)} %bitcast.125, bf16[176,2048]{1,0:T(8,128)(2,1)S(1)} %bitcast.128, bf16[640,512]{1,0:T(8,128)(2,1)S(1)} %get-tuple-element.29, bf16[640,512]{1,0:T(8,128)(2,1)S(1)} %get-tuple-element.30, ...), kind=kOutput, calls=%fused_computation.31 | convolution fusion | flops 1864630272 | bytes 7307264 | tf_op jit(solution)/shard_map/dot_general | solution.py:17
  110.1 19.7 %all-to-all-done.1 = bf16[4,640,512]{2,1,0:T(8,128)(2,1)} async-done(((bf16[4,640,512]{2,1,0:T(8,128)(2,1)}), bf16[4,640,512]{2,1,0:T(8,128)(2,1)}, u32[]{:S(2)}, u32[]{:S(2)}) %all-to-all-start.1) | async-done | bytes 2621472 | tf_op jit(solution)/shard_map/all_to_all | solution.py:43
  129.9 2.0 slice_bitcast_fusion.7
  132.0 2.3 %fusion.20 = (bf16[640,352]{0,1:T(8,128)(2,1)S(1)}, f32[640]{0:T(1024)S(1)}, bf16[640,352]{0,1:T(8,128)(2,1)}) fusion(f32[640,2,1,176]{0,3,2,1:T(8,128)S(1)} %get-tuple-element.37, f32[640,2,1,176]{0,3,2,1:T(8,128)S(1)} %get-tuple-element.38, bf16[176,2048]{1,0:T(8,128)(2,1)S(1)} %copy-done.11, bf16[176,2048]{1,0:T(8,128)(2,1)S(1)} %bitcast.122, ...), kind=kOutput, calls=%fused_computation.53 | convolution fusion | flops 939720064 | bytes 6769152 | tf_op jit(solution)/shard_map/dot_general | solution.py:17
  134.4 1.2 fusion.79
  135.6 3.7 %convolution_convert_fusion = bf16[640,2048]{1,0:T(8,128)(2,1)S(1)} fusion(bf16[352,2048]{1,0:T(8,128)(2,1)S(1)} %copy-done.10, bf16[176,2048]{1,0:T(8,128)(2,1)} %bitcast.124, bf16[176,2048]{1,0:T(8,128)(2,1)} %bitcast.127, bf16[640,176]{0,1:T(8,128)(2,1)S(1)} %get-tuple-element.48, bf16[640,176]{0,1:T(8,128)(2,1)S(1)} %get-tuple-element.46, ...), kind=kOutput, calls=%fused_computation.1 | convolution fusion | flops 1859059712 | bytes 6406144 | tf_op jit(solution)/shard_map/dot_general | solution.py:17
  139.9 1.9 pad_maximum_fusion.1
  141.8 4.0 %all-to-all-start.3 = ((bf16[4,648,512]{2,1,0:T(8,128)(2,1)}), bf16[4,648,512]{2,1,0:T(8,128)(2,1)S(1)}, u32[]{:S(2)}, u32[]{:S(2)}) async-start(bf16[4,648,512]{2,1,0:T(8,128)(2,1)} %pad_maximum_fusion.1), calls=%async_computation.3 | async-start | bytes 5308416 | tf_op jit(solution)/shard_map/all_to_all | solution.py:43
  145.7 1.7 bitcast_multiply_fusion.2
  147.5 2.9 %fusion.31 = f32[352,2048]{1,0:T(8,128)S(1)} fusion(bf16[640,352]{0,1:T(8,128)(2,1)S(1)} %bitcast_multiply_fusion.2, bf16[640,512]{1,0:T(8,128)(2,1)} %copy-done.26, bf16[640,512]{1,0:T(8,128)(2,1)} %copy-done.27, bf16[640,512]{1,0:T(8,128)(2,1)} %copy-done.28, bf16[640,512]{1,0:T(8,128)(2,1)S(1)} %copy-done.25), kind=kOutput, calls=%fused_computation.79 | convolution fusion | flops 933232640 | bytes 5955584 | tf_op jit(solution)/shard_map/dot_general | solution.py:17
  150.5 1.6 copy-done.7
  152.3 2.4 %fusion.33 = f32[704,2048]{1,0:T(8,128)S(1)} fusion(bf16[640,512]{1,0:T(8,128)(2,1)S(1)} %copy-done.19, bf16[640,512]{1,0:T(8,128)(2,1)S(1)} %copy-done.21, bf16[640,512]{1,0:T(8,128)(2,1)S(1)} %copy-done.23, bf16[640,512]{1,0:T(8,128)(2,1)S(1)} %copy-done.17, bf16[640,176]{0,1:T(8,128)(2,1)S(1)} %copy-done.36, bf16[640,176]{0,1:T(8,128)(2,1)S(1)} %copy-done.32, ...), kind=kOutput, calls=%fused_computation.81 | convolution fusion | flops 1859584000 | bytes 9289728 | tf_op jit(solution)/shard_map/dot_general | solution.py:17
  154.9 2.1 pad_maximum_fusion.5
  157.8 1.9 collective-permute-start.1
  159.7 13.5 %all-to-all-done.3 = bf16[4,648,512]{2,1,0:T(8,128)(2,1)S(1)} async-done(((bf16[4,648,512]{2,1,0:T(8,128)(2,1)}), bf16[4,648,512]{2,1,0:T(8,128)(2,1)S(1)}, u32[]{:S(2)}, u32[]{:S(2)}) %all-to-all-start.3) | async-done | bytes 2654240 | tf_op jit(solution)/shard_map/all_to_all | solution.py:43
  174.9 1.4 convert.11
  179.0 14.4 %all-to-all-start.4 = ((bf16[64,8,768]{2,1,0:T(8,128)(2,1)}), bf16[64,8,768]{2,1,0:T(8,128)(2,1)S(1)}, u32[]{:S(2)}, u32[]{:S(2)}) async-start(bf16[64,8,768]{2,1,0:T(8,128)(2,1)} %fusion.21), calls=%async_computation.4 | async-start | bytes 1572864 | tf_op jit(solution)/shard_map/all_to_all | solution.py:27
  193.4 2.3 %convert_element_type.165 = f32[528,2048]{1,0:T(8,128)S(1)} convert(bf16[528,2048]{1,0:T(8,128)(2,1)} %collective-permute-done.1) | non-fusion elementwise | flops 1081344 | bytes 6488064 | tf_op jit(solution)/shard_map/convert_element_type | solution.py:188
  195.8 3.5 %fusion.23 = (bf16[1,176,2048]{2,1,0:T(8,128)(2,1)}, bf16[1,176,2048]{2,1,0:T(8,128)(2,1)}, bf16[1,176,2048]{2,1,0:T(8,128)(2,1)}) fusion(f32[528,2048]{1,0:T(8,128)S(1)} %convert_element_type.165, f32[704,2048]{1,0:T(8,128)} %copy-done.5, f32[352,2048]{1,0:T(8,128)S(1)} %copy-done.8), kind=kLoop, calls=%fused_computation.60 | loop fusion | flops 2162688 | bytes 10813440 | tf_op jit(solution)/shard_map/broadcast_in_dim | solution.py:190
  199.4 16.1 %all-to-all-done.4 = bf16[64,8,768]{2,1,0:T(8,128)(2,1)S(1)} async-done(((bf16[64,8,768]{2,1,0:T(8,128)(2,1)}), bf16[64,8,768]{2,1,0:T(8,128)(2,1)S(1)}, u32[]{:S(2)}, u32[]{:S(2)}) %all-to-all-start.4) | async-done | bytes 786464 | tf_op jit(solution)/shard_map/all_to_all | solution.py:27
  (144 shorter events, 15.8 us)
Async XLA Ops:
  61.6 4.4 %copy-start.12 = (bf16[1,176,2048]{2,1,0:T(8,128)(2,1)S(1)}, bf16[1,176,2048]{2,1,0:T(8,128)(2,1)}, u32[]{:S(2)}) copy-start(bf16[1,176,2048]{2,1,0:T(8,128)(2,1)} %param.13) | copy-start | bytes 2162692
  61.6 33.6 %all-to-all-start.2 = ((bf16[4,640,512]{2,1,0:T(8,128)(2,1)}), bf16[4,640,512]{2,1,0:T(8,128)(2,1)S(1)}, u32[]{:S(2)}, u32[]{:S(2)}) async-start(bf16[4,640,512]{2,1,0:T(8,128)(2,1)} %broadcast_in_dim.151), calls=%async_computation.2 | async-start | bytes 5242880 | tf_op jit(solution)/shard_map/all_to_all | solution.py:43
  66.0 4.9 %copy-start.6 = (bf16[512,512]{1,0:T(8,128)(2,1)S(1)}, bf16[512,512]{1,0:T(8,128)(2,1)}, u32[]{:S(2)}) copy-start(bf16[512,512]{1,0:T(8,128)(2,1)} %get-tuple-element.40) | copy-start | bytes 1572868
  68.9 32.6 %collective-permute-start = (bf16[528,2048]{1,0:T(8,128)(2,1)}, bf16[528,2048]{1,0:T(8,128)(2,1)}, u32[]{:S(2)}, u32[]{:S(2)}) collective-permute-start(bf16[528,2048]{1,0:T(8,128)(2,1)} %pad_maximum_fusion.4), channel_id=1, source_target_pairs={{0,4},{4,0},{8,12},{12,8},{16,20},{20,16},{24,28},{28,24},{32,36},... | collective-permute-start | bytes 6488072 | tf_op jit(solution)/shard_map/ppermute | solution.py:39
  96.9 32.9 %all-to-all-start.1 = ((bf16[4,640,512]{2,1,0:T(8,128)(2,1)}), bf16[4,640,512]{2,1,0:T(8,128)(2,1)}, u32[]{:S(2)}, u32[]{:S(2)}) async-start(bf16[4,640,512]{2,1,0:T(8,128)(2,1)} %broadcast_in_dim.150), calls=%async_computation.1 | async-start | bytes 5242880 | tf_op jit(solution)/shard_map/all_to_all | solution.py:43
  105.3 4.6 %copy-start.16 = (bf16[640,512]{1,0:T(8,128)(2,1)}, bf16[640,512]{1,0:T(8,128)(2,1)S(1)}, u32[]{:S(2)}) copy-start(bf16[640,512]{1,0:T(8,128)(2,1)S(1)} %get-tuple-element.28) | copy-start | bytes 1966084
  105.3 4.6 %copy-start.18 = (bf16[640,512]{1,0:T(8,128)(2,1)}, bf16[640,512]{1,0:T(8,128)(2,1)S(1)}, u32[]{:S(2)}) copy-start(bf16[640,512]{1,0:T(8,128)(2,1)S(1)} %get-tuple-element.29) | copy-start | bytes 1966084
  105.3 4.6 %copy-start.20 = (bf16[640,512]{1,0:T(8,128)(2,1)}, bf16[640,512]{1,0:T(8,128)(2,1)S(1)}, u32[]{:S(2)}) copy-start(bf16[640,512]{1,0:T(8,128)(2,1)S(1)} %get-tuple-element.30) | copy-start | bytes 1966084
  105.3 4.6 %copy-start.22 = (bf16[640,512]{1,0:T(8,128)(2,1)}, bf16[640,512]{1,0:T(8,128)(2,1)S(1)}, u32[]{:S(2)}) copy-start(bf16[640,512]{1,0:T(8,128)(2,1)S(1)} %get-tuple-element.31) | copy-start | bytes 1966084
  110.1 21.8 %copy-start.3 = (f32[640,2,1,176]{0,3,2,1:T(8,128)}, f32[640,2,1,176]{0,3,2,1:T(8,128)S(1)}, u32[]{:S(2)}) copy-start(f32[640,2,1,176]{0,3,2,1:T(8,128)S(1)} %get-tuple-element.37) | copy-start | bytes 2703364
  110.1 21.8 %copy-start.4 = (f32[640,2,1,176]{0,3,2,1:T(8,128)}, f32[640,2,1,176]{0,3,2,1:T(8,128)S(1)}, u32[]{:S(2)}) copy-start(f32[640,2,1,176]{0,3,2,1:T(8,128)S(1)} %get-tuple-element.38) | copy-start | bytes 2703364
  132.0 3.6 %copy-start.10 = (bf16[352,2048]{1,0:T(8,128)(2,1)S(1)}, bf16[352,2048]{1,0:T(8,128)(2,1)}, u32[]{:S(2)}) copy-start(bf16[352,2048]{1,0:T(8,128)(2,1)} %copy-done.9) | copy-start | bytes 4325380
  134.3 5.0 %copy-start.29 = (bf16[640,176]{0,1:T(8,128)(2,1)}, bf16[640,176]{0,1:T(8,128)(2,1)S(1)}, u32[]{:S(2)}) copy-start(bf16[640,176]{0,1:T(8,128)(2,1)S(1)} %get-tuple-element.45) | copy-start | bytes 675844
  134.3 5.0 %copy-start.31 = (bf16[640,176]{0,1:T(8,128)(2,1)}, bf16[640,176]{0,1:T(8,128)(2,1)S(1)}, u32[]{:S(2)}) copy-start(bf16[640,176]{0,1:T(8,128)(2,1)S(1)} %get-tuple-element.46) | copy-start | bytes 675844
  135.6 3.8 %copy-start.33 = (bf16[640,176]{0,1:T(8,128)(2,1)}, bf16[640,176]{0,1:T(8,128)(2,1)S(1)}, u32[]{:S(2)}) copy-start(bf16[640,176]{0,1:T(8,128)(2,1)S(1)} %get-tuple-element.47) | copy-start | bytes 675844
  135.6 3.8 %copy-start.35 = (bf16[640,176]{0,1:T(8,128)(2,1)}, bf16[640,176]{0,1:T(8,128)(2,1)S(1)}, u32[]{:S(2)}) copy-start(bf16[640,176]{0,1:T(8,128)(2,1)S(1)} %get-tuple-element.48) | copy-start | bytes 675844
  141.8 5.7 %copy-start.25 = (bf16[640,512]{1,0:T(8,128)(2,1)S(1)}, bf16[640,512]{1,0:T(8,128)(2,1)}, u32[]{:S(2)}) copy-start(bf16[640,512]{1,0:T(8,128)(2,1)} %copy-done.24) | copy-start | bytes 1966084
  141.8 31.5 %all-to-all-start.3 = ((bf16[4,648,512]{2,1,0:T(8,128)(2,1)}), bf16[4,648,512]{2,1,0:T(8,128)(2,1)S(1)}, u32[]{:S(2)}, u32[]{:S(2)}) async-start(bf16[4,648,512]{2,1,0:T(8,128)(2,1)} %pad_maximum_fusion.1), calls=%async_computation.3 | async-start | bytes 5308416 | tf_op jit(solution)/shard_map/all_to_all | solution.py:43
  147.5 4.7 %copy-start.17 = (bf16[640,512]{1,0:T(8,128)(2,1)S(1)}, bf16[640,512]{1,0:T(8,128)(2,1)}, u32[]{:S(2)}) copy-start(bf16[640,512]{1,0:T(8,128)(2,1)} %copy-done.16) | copy-start | bytes 1966084
  147.5 4.7 %copy-start.19 = (bf16[640,512]{1,0:T(8,128)(2,1)S(1)}, bf16[640,512]{1,0:T(8,128)(2,1)}, u32[]{:S(2)}) copy-start(bf16[640,512]{1,0:T(8,128)(2,1)} %copy-done.18) | copy-start | bytes 1966084
  147.5 4.7 %copy-start.21 = (bf16[640,512]{1,0:T(8,128)(2,1)S(1)}, bf16[640,512]{1,0:T(8,128)(2,1)}, u32[]{:S(2)}) copy-start(bf16[640,512]{1,0:T(8,128)(2,1)} %copy-done.20) | copy-start | bytes 1966084
  147.5 4.7 %copy-start.23 = (bf16[640,512]{1,0:T(8,128)(2,1)S(1)}, bf16[640,512]{1,0:T(8,128)(2,1)}, u32[]{:S(2)}) copy-start(bf16[640,512]{1,0:T(8,128)(2,1)} %copy-done.22) | copy-start | bytes 1966084
  147.5 4.7 %copy-start.30 = (bf16[640,176]{0,1:T(8,128)(2,1)S(1)}, bf16[640,176]{0,1:T(8,128)(2,1)}, u32[]{:S(2)}) copy-start(bf16[640,176]{0,1:T(8,128)(2,1)} %copy-done.29) | copy-start | bytes 675844
  147.5 4.7 %copy-start.32 = (bf16[640,176]{0,1:T(8,128)(2,1)S(1)}, bf16[640,176]{0,1:T(8,128)(2,1)}, u32[]{:S(2)}) copy-start(bf16[640,176]{0,1:T(8,128)(2,1)} %copy-done.31) | copy-start | bytes 675844
  147.5 4.7 %copy-start.34 = (bf16[640,176]{0,1:T(8,128)(2,1)S(1)}, bf16[640,176]{0,1:T(8,128)(2,1)}, u32[]{:S(2)}) copy-start(bf16[640,176]{0,1:T(8,128)(2,1)} %copy-done.33) | copy-start | bytes 675844
  147.5 4.7 %copy-start.36 = (bf16[640,176]{0,1:T(8,128)(2,1)S(1)}, bf16[640,176]{0,1:T(8,128)(2,1)}, u32[]{:S(2)}) copy-start(bf16[640,176]{0,1:T(8,128)(2,1)} %copy-done.35) | copy-start | bytes 675844
  157.8 35.6 %collective-permute-start.1 = (bf16[528,2048]{1,0:T(8,128)(2,1)}, bf16[528,2048]{1,0:T(8,128)(2,1)}, u32[]{:S(2)}, u32[]{:S(2)}) collective-permute-start(bf16[528,2048]{1,0:T(8,128)(2,1)} %pad_maximum_fusion.5), channel_id=1, source_target_pairs={{0,4},{4,0},{8,12},{12,8},{16,20},{20,16},{24,28},{28,24},{32,36},... | collective-permute-start | bytes 6488072 | tf_op jit(solution)/shard_map/ppermute | solution.py:39
  179.0 36.5 %all-to-all-start.4 = ((bf16[64,8,768]{2,1,0:T(8,128)(2,1)}), bf16[64,8,768]{2,1,0:T(8,128)(2,1)S(1)}, u32[]{:S(2)}, u32[]{:S(2)}) async-start(bf16[64,8,768]{2,1,0:T(8,128)(2,1)} %fusion.21), calls=%async_computation.4 | async-start | bytes 1572864 | tf_op jit(solution)/shard_map/all_to_all | solution.py:27
  195.8 20.4 %copy-start.38 = (f32[128,64]{0,1:T(8,128)S(1)}, f32[128,64]{0,1:T(8,128)}, u32[]{:S(2)}) copy-start(f32[128,64]{0,1:T(8,128)} %copy-done.37) | copy-start | bytes 98308
  195.8 20.5 %copy-start.39 = (s32[128,4]{0,1:T(4,128)S(1)}, s32[128,4]{0,1:T(4,128)}, u32[]{:S(2)}) copy-start(s32[128,4]{0,1:T(4,128)} %param.9) | copy-start | bytes 6148
  195.8 20.6 %copy-start.40 = (bf16[128,4]{0,1:T(4,128)(2,1)S(1)}, bf16[128,4]{0,1:T(4,128)(2,1)}, u32[]{:S(2)}) copy-start(bf16[128,4]{0,1:T(4,128)(2,1)} %param.10) | copy-start | bytes 3076
  195.8 22.0 %copy-start.1 = (bf16[128,512]{1,0:T(8,128)(2,1)S(1)}, bf16[128,512]{1,0:T(8,128)(2,1)}, u32[]{:S(2)}) copy-start(bf16[128,512]{1,0:T(8,128)(2,1)} %param.8) | copy-start | bytes 393220
  (15 other events, 32.4 us)

commit v2 on v0

v2 whole, which is shorter than its diff:
```python
import functools

import jax
import jax.numpy as jnp
from jax import lax
from jax.experimental import pallas as pl
from jax.experimental.pallas import tpu as pltpu
from jax.sharding import PartitionSpec as P

CAPACITY = 10
SHARE = CAPACITY // 2
HEAD = 4
TILE = 8
FOLDS = TILE // HEAD
LANES = 128
EXTRA = 16

bf16 = jnp.bfloat16
f32 = jnp.float32


def dot_f32(left, right, left_dim, right_dim):
    return lax.dot_general(
        left, right, (((left_dim,), (right_dim,)), ((), ())), preferred_element_type=f32
    )


def local_call(body, out_shape, *operands):
    return pl.pallas_call(
        body,
        out_shape=out_shape,
        compiler_params=pltpu.CompilerParams(vmem_limit_bytes=48 * 1024 * 1024),
    )(*operands)


def shape(rows, columns, dtype):
    return jax.ShapeDtypeStruct((rows, columns), dtype)


def iota(rows, columns, dim):
    return lax.broadcasted_iota(jnp.int32, (rows, columns), dim)


def exchange_chips(block):
    devices = lax.axis_size("ep")
    return lax.all_to_all(
        block,
        "ep",
        split_axis=0,
        concat_axis=0,
        axis_index_groups=[list(range(core, devices, 2)) for core in range(2)],
        tiled=True,
    )


def other_core(value):
    pairs = [(source, source ^ 1) for source in range(lax.axis_size("ep"))]
    return lax.ppermute(value, "ep", pairs)


def row_partner(value):
    count = lax.axis_size("et")
    return lax.ppermute(value, "et", [(source, count - 1 - source) for source in range(count)])


def unit_partner(value):
    pairs = [(source, source ^ 1) for source in range(lax.axis_size("et"))]
    return lax.ppermute(value, "et", pairs)


def is_upper():
    return lax.axis_index("et") >= 2


def is_outer():
    index = lax.axis_index("et")
    return (index == 0) | (index == 3)


def hit_of(ids, top, experts):
    return ids[:, top : top + 1] == iota(ids.shape[0], experts, 1)


def place_codes(ids, experts, upper):
    tokens, top_count = ids.shape
    hit = sum(hit_of(ids, top, experts).astype(f32) for top in range(top_count))
    earlier = (iota(tokens, tokens, 1) < iota(tokens, tokens, 0)).astype(f32).astype(bf16)
    rank = dot_f32(earlier, hit.astype(bf16), 1, 0)
    shift = jnp.where(upper, float(SHARE), 0.0)
    return jnp.where(hit > 0.0, rank - shift, 255.0)


def as_mask(condition):
    return jnp.where(condition, 1.0, 0.0)


def pack_kernel(ids_ref, probs_ref, own_x_ref, own_dy_ref, got_ref, send_ref):
    ids = ids_ref[...]
    tokens, top_count = ids.shape
    quarter = own_x_ref.shape[1]
    wide = send_ref.shape[0]
    experts = wide // TILE
    upper = is_upper()
    code = place_codes(ids, experts, upper)
    probs = probs_ref[...].astype(f32)
    weight = sum(
        jnp.where(hit_of(ids, top, experts), probs[:, top : top + 1], 0.0)
        for top in range(top_count)
    )
    spread = as_mask(iota(wide, experts, 0) // TILE == iota(wide, experts, 1)).astype(bf16)
    wide_code = dot_f32(spread, code.astype(bf16), 1, 1)
    wide_weight = dot_f32(spread, weight.astype(bf16), 1, 1)
    row = iota(wide, tokens, 0) % TILE
    head = wide_code == (row % HEAD).astype(f32)
    rest = wide_code == float(HEAD)
    edge = quarter + FOLDS * quarter // TILE

    def place(first, second, scale, start):
        main = jnp.zeros((wide, quarter), f32)
        tail = jnp.zeros((wide, LANES), f32)
        for fold, part in enumerate((first, second)):
            pick = jnp.where(head & (row // HEAD == fold), scale, 0.0).astype(bf16)
            main += dot_f32(pick, part, 1, 0)
            for index in range(HEAD):
                pick = jnp.where(rest & (row == fold * HEAD + index), scale, 0.0).astype(bf16)
                tail += dot_f32(pick, part[:, index * LANES : (index + 1) * LANES], 1, 0)
        send_ref[:, start : start + quarter] = main.astype(bf16)
        send_ref[:, start + quarter : start + edge] = tail.astype(bf16)

    own_x, own_dy = own_x_ref[...], own_dy_ref[...]
    got_x, got_dy = got_ref[:tokens], got_ref[tokens:]
    place(
        jnp.where(upper, got_x, own_x),
        jnp.where(upper, own_x, got_x),
        jnp.ones((wide, tokens), f32),
        0,
    )
    place(
        jnp.where(upper, got_dy, own_dy), jnp.where(upper, own_dy, got_dy), wide_weight, edge
    )


def unpack_kernel(mine_ref, theirs_ref, full_ref):
    wide = mine_ref.shape[0]
    quarter = full_ref.shape[1] // 4
    experts = wide // TILE
    heads = experts * HEAD
    outer = is_outer()
    mine, theirs = mine_ref[...], theirs_ref[...]
    slot = iota(heads, wide, 0)
    source = iota(heads, wide, 1)
    rest_slot = iota(experts, wide, 0)
    rest_source = iota(experts, wide, 1)
    places = ((0, 3), (1, 2))
    for side, columns in enumerate(places):
        block = jnp.where(outer, mine, theirs) if side == 0 else jnp.where(outer, theirs, mine)
        for fold, column in enumerate(columns):
            pick = as_mask(source == slot // HEAD * TILE + fold * HEAD + slot % HEAD).astype(bf16)
            full_ref[:heads, column * quarter : (column + 1) * quarter] = dot_f32(
                pick, block[:, :quarter], 1, 0
            ).astype(bf16)
            for index in range(HEAD):
                pick = as_mask(rest_source == rest_slot * TILE + fold * HEAD + index).astype(bf16)
                start = column * quarter + index * LANES
                full_ref[heads:, start : start + LANES] = dot_f32(
                    pick, block[:, quarter:], 1, 0
                ).astype(bf16)


def back_kernel(half, pre_ref, down_ref, joint_ref, hidden_ref, prob_ref):
    slots = pre_ref.shape[0]
    ones = jnp.ones((EXTRA, half), bf16)
    total = jnp.zeros((EXTRA, slots), f32)
    for part in range(2):
        start = 2 * half * part
        pre_gate = pre_ref[:, start : start + half]
        pre_up = pre_ref[:, start + half : start + 2 * half]
        down_back = down_ref[:, half * part : half * (part + 1)]
        sigmoid = jax.nn.sigmoid(pre_gate)
        silu_value = pre_gate * sigmoid
        hidden = silu_value * pre_up
        slope = sigmoid * (1.0 + pre_gate * (1.0 - sigmoid))
        joint_ref[:, start : start + half] = (down_back * pre_up * slope).astype(bf16)
        joint_ref[:, start + half : start + 2 * half] = (down_back * silu_value).astype(bf16)
        hidden_ref[:, half * part : half * (part + 1)] = hidden.astype(bf16)
        product = hidden * down_back
        high = product.astype(bf16)
        low = (product - high.astype(f32)).astype(bf16)
        total += dot_f32(ones, high, 1, 1) + dot_f32(ones, low, 1, 1)
    high = total.astype(bf16)
    low = (total - high.astype(f32)).astype(bf16)
    row = iota(EXTRA, slots, 0)
    zero = jnp.zeros_like(high)
    prob_ref[...] = jnp.zeros_like(prob_ref)
    prob_ref[:, :slots] = jnp.where(row == 0, high, jnp.where(row == 1, low, zero))


def give_kernel(block_ref, prob_ref, got_ref, give_ref):
    slots = block_ref.shape[0]
    quarter = block_ref.shape[1] // 4
    wide = give_ref.shape[0]
    experts = wide // TILE
    heads = experts * HEAD
    outer = is_outer()
    slot = iota(wide, heads, 1)
    target = iota(wide, heads, 0)
    rest_slot = iota(wide, experts, 1)
    rest_target = iota(wide, experts, 0)
    main = jnp.zeros((wide, quarter), f32)
    tail = jnp.zeros((wide, LANES), f32)
    for fold, (outside, inside) in enumerate(((0, 1), (3, 2))):
        kept = jnp.where(
            outer,
            block_ref[:, outside * quarter : (outside + 1) * quarter],
            block_ref[:, inside * quarter : (inside + 1) * quarter],
        )
        got = got_ref[:slots, fold * quarter : (fold + 1) * quarter]
        route = (kept.astype(f32) + got.astype(f32)).astype(bf16)
        pick = as_mask(target == slot // HEAD * TILE + fold * HEAD + slot % HEAD).astype(bf16)
        main += dot_f32(pick, route[:heads], 1, 0)
        for index in range(HEAD):
            pick = as_mask(rest_target == rest_slot * TILE + fold * HEAD + index).astype(bf16)
            tail += dot_f32(pick, route[heads:, index * LANES : (index + 1) * LANES], 1, 0)
    give_ref[:, :quarter] = main.astype(bf16)
    give_ref[:, quarter : quarter + LANES] = tail.astype(bf16)
    both = prob_ref[:, :slots].astype(f32) + got_ref[slots:, :slots].astype(f32)
    total = jnp.sum(both, axis=0, keepdims=True)
    high = total.astype(bf16).astype(f32)
    rows = iota(LANES, slots, 0)
    spread = jnp.where(rows == 0, high, jnp.where(rows == 1, total - high, 0.0)).astype(bf16)
    place = iota(wide, slots, 0)
    column = iota(wide, slots, 1)
    row = place % TILE
    expected = jnp.where(row < HEAD, place // TILE * HEAD + row, heads + place // TILE)
    pick = as_mask((column == expected) & (row < SHARE)).astype(bf16)
    give_ref[:, quarter + LANES :] = dot_f32(pick, spread, 1, 1).astype(bf16)


def combine_kernel(ids_ref, back_ref, own_ref, pass_ref):
    ids = ids_ref[...]
    tokens = ids.shape[0]
    quarter = own_ref.shape[1]
    wide = back_ref.shape[0]
    experts = wide // TILE
    upper = is_upper()
    code = place_codes(ids, experts, upper)
    spread = as_mask(iota(experts, wide, 0) == iota(experts, wide, 1) // TILE).astype(bf16)
    wide_code = dot_f32(code.astype(bf16), spread, 1, 0)
    row = iota(tokens, wide, 1) % TILE
    head = wide_code == (row % HEAD).astype(f32)
    rest = wide_code == float(HEAD)
    back_main = back_ref[:, :quarter]
    back_tail = back_ref[:, quarter : quarter + LANES]
    sums = []
    for fold in range(FOLDS):
        pick = as_mask(head & (row // HEAD == fold)).astype(bf16)
        tails = []
        for index in range(HEAD):
            tail_pick = as_mask(rest & (row == fold * HEAD + index)).astype(bf16)
            tails.append(dot_f32(tail_pick, back_tail, 1, 0))
        sums.append(dot_f32(pick, back_main, 1, 0) + jnp.concatenate(tails, axis=1))
    own_ref[...] = jnp.where(upper, sums[1], sums[0])
    pass_ref[:, :quarter] = jnp.where(upper, sums[0], sums[1]).astype(bf16)
    columns = back_ref[:, quarter + LANES :].astype(f32)
    lane = iota(wide, LANES, 1)
    expert = iota(wide, LANES, 0) // TILE
    by_lane = jnp.where(lane == expert, columns[:, 0:1], 0.0)
    by_lane += jnp.where(lane == expert + LANES // 2, columns[:, 1:2], 0.0)
    pick = as_mask(wide_code == row.astype(f32)).astype(bf16)
    pass_ref[:, quarter:] = dot_f32(pick, by_lane.astype(bf16), 1, 0).astype(bf16)


def finish_kernel(ids_ref, probs_ref, own_ref, pass_ref, got_ref, input_ref, prob_ref):
    ids = ids_ref[...]
    tokens, top_count = ids.shape
    quarter = own_ref.shape[1]
    input_ref[...] = (own_ref[...] + got_ref[:, :quarter].astype(f32)).astype(bf16)
    total = pass_ref[:, quarter:].astype(f32) + got_ref[:, quarter:].astype(f32)
    expert = iota(tokens, LANES, 1) % (LANES // 2)
    chosen = [
        jnp.sum(jnp.where(ids[:, top : top + 1] == expert, total, 0.0), axis=1, keepdims=True)
        for top in range(top_count)
    ]
    prob_ref[...] = jnp.concatenate(chosen, axis=1) / probs_ref[...].astype(f32)


def shards(activations, cotangent, expert_ids, route_probs, gate_weight, up_weight, down_weight):
    tokens, quarter = activations.shape
    experts = lax.axis_size("ep") // 2
    units = gate_weight.shape[1]
    wide = experts * TILE
    slots = experts * SHARE
    edge = quarter + LANES
    outer = is_outer()

    got_tokens = row_partner(jnp.concatenate([activations, cotangent], axis=0))
    own_weights = jnp.concatenate([gate_weight[0], up_weight[0], down_weight[0]], axis=0)
    got_tokens, own_weights = lax.optimization_barrier((got_tokens, own_weights))
    far_weights = row_partner(own_weights)
    own_twin = other_core(own_weights)
    far_twin = other_core(far_weights)

    send = local_call(
        pack_kernel,
        shape(wide, 2 * edge, bf16),
        expert_ids,
        route_probs,
        activations,
        cotangent,
        got_tokens,
    )
    got = exchange_chips(send.reshape(experts, TILE, 2 * edge))
    half = -(-2 * units // LANES) * LANES
    gap = jnp.zeros((half - 2 * units, 4 * quarter), bf16)

    def joined(index):
        part = slice(index * units, (index + 1) * units)
        return (
            [far_weights[part], far_twin[part], gap],
            [own_weights[part], own_twin[part], gap],
        )

    (far_gate, own_gate), (far_up, own_up), (far_down, own_down) = joined(0), joined(1), joined(2)
    wide_all = jnp.concatenate(far_gate + far_up + own_gate + own_up, axis=0)
    down_all = jnp.concatenate(far_down + own_down, axis=0)
    rows = got[:, :, :edge].reshape(wide, edge)
    grads = got[:, :, edge:].reshape(wide, edge)
    full = shape(slots, 4 * quarter, bf16)
    their_rows = unit_partner(rows)
    their_grads = unit_partner(grads)
    their_rows, wide_all, down_all = lax.optimization_barrier((their_rows, wide_all, down_all))
    full_rows = local_call(unpack_kernel, full, rows, their_rows)
    full_grads = local_call(unpack_kernel, full, grads, their_grads)
    pre = dot_f32(full_rows, wide_all, 1, 1)
    down_back = dot_f32(full_grads, down_all, 1, 1)
    joint, hidden, prob = local_call(
        functools.partial(back_kernel, half),
        (
            shape(slots, 4 * half, bf16),
            shape(slots, 2 * half, bf16),
            shape(EXTRA, 2 * quarter, bf16),
        ),
        pre,
        down_back,
    )
    block = dot_f32(joint, wide_all, 1, 0).astype(bf16)
    outside = jnp.concatenate([block[:, :quarter], block[:, 3 * quarter :]], axis=1)
    inside = block[:, quarter : 3 * quarter]
    given = jnp.concatenate([jnp.where(outer, inside, outside), prob], axis=0)
    taken = unit_partner(given)
    given, joint_late, hidden_late = lax.optimization_barrier((given, joint, hidden))

    def unit_grads(part):
        wide_part = dot_f32(joint_late[:, 2 * half * part : 2 * half * (part + 1)], full_rows, 0, 0)
        down_part = dot_f32(hidden_late[:, half * part : half * (part + 1)], full_grads, 0, 0)
        wide_part, down_part = wide_part.astype(bf16), down_part.astype(bf16)
        starts = ((wide_part, 0), (wide_part, half), (down_part, 0))
        kept = jnp.concatenate([a[s : s + units] for a, s in starts], axis=0)
        sent = jnp.concatenate([a[s + units : s + 2 * units] for a, s in starts], axis=0)
        return kept.astype(f32) + other_core(sent).astype(f32)

    far_grads = unit_grads(0).astype(bf16)
    far_got = row_partner(far_grads)
    taken, far_grads = lax.optimization_barrier((taken, far_grads))
    own_grads = (unit_grads(1) + far_got.astype(f32)).astype(bf16)

    give = local_call(give_kernel, shape(wide, edge + LANES, bf16), block, prob, taken)
    back = exchange_chips(give.reshape(experts, TILE, edge + LANES)).reshape(wide, edge + LANES)
    own_sum, passed = local_call(
        combine_kernel,
        (shape(tokens, quarter, f32), shape(tokens, quarter + LANES, bf16)),
        expert_ids,
        back,
    )
    input_grad, prob_grad = local_call(
        finish_kernel,
        (shape(tokens, quarter, bf16), shape(tokens, expert_ids.shape[1], f32)),
        expert_ids,
        route_probs,
        own_sum,
        passed,
        row_partner(passed),
    )
    return (
        input_grad,
        prob_grad,
        own_grads[:units][None],
        own_grads[units : 2 * units][None],
        own_grads[2 * units :][None],
    )


def solution(mesh):
    placed = (
        P("ep", "et"),
        P("ep", "et"),
        P("ep", None),
        P("ep", None),
        P("ep", "et", None),
        P("ep", "et", None),
        P("ep", "et", None),
    )
    return jax.shard_map(
        shards,
        mesh=mesh,
        in_specs=placed,
        out_specs=(
            P("ep", "et"),
            P("ep", None),
            P("ep", "et", None),
            P("ep", "et", None),
            P("ep", "et", None),
        ),
        check_vma=False,
    )
```

time: 373 us -> 202 us (0.54)
  the two profiles are of different devices: /device:TPU:1 before, /device:TPU:24 now
where the time goes in v2:
time: 202 us; the launch traced here: 201 us
  waiting for transfers between devices  56.4 us (28%)
  starting transfers between devices  49.1 us (24%)
  blocking collectives  35.2 us (17%)
  local copies, waits for them, and re-layouts  21.1 us (10%)
  matrix products  16.9 us (8%)
  other arithmetic  12.3 us (6%)
  Pallas kernels  9 us (4%)
    ppermute x4, waiting for transfers between devices, row_partner(): lax.ppermute(value, 'et', [(source, count - 1 - source) for source in ran...  36.4 us
    all_to_all x1, blocking collectives, exchange_chips(): lax.all_to_all(block, 'ep', split_axis=0, concat_axis=0, axis_index_group...  35.2 us
    unnamed x22, local copies, waits for them, and re-layouts  18.2 us
    dot_general x7, matrix products, dot_f32(): lax.dot_general(left, right, (((left_dim,), (right_dim,)), ((), ())), pre...  16.9 us
    all_to_all x1, starting transfers between devices, exchange_chips(): lax.all_to_all(block, 'ep', split_axis=0, concat_axis=0, axis_index_group...  16.4 us
    ppermute x4, starting transfers between devices, row_partner(): lax.ppermute(value, 'et', [(source, count - 1 - source) for source in ran...  16.4 us
    ppermute x3, waiting for transfers between devices, unit_partner(): return lax.ppermute(value, 'et', pairs)  15 us
    pallas_call x7, Pallas kernels, local_call(): pl.pallas_call(body, out_shape=out_shape, compiler_params=pltpu.CompilerP...  9 us
  transfers between devices with their start and end apart: 12, of which 6 were waited for; matrix products, arithmetic and copies ran while one was open for 15% of the time, Pallas kernels for 4%

profile of v2, /device:TPU:24, one launch (start us, length us, event | category | flops | bytes accessed | tf_op | source)
XLA Modules:
  0.0 201.0 jit_solution(12794435341502872644)
XLA Ops:
  1.7 4.7 %collective-permute-start = (bf16[256,512]{1,0:T(8,128)(2,1)S(1)}, bf16[256,512]{1,0:T(8,128)(2,1)S(1)}, u32[]{:S(2)}, u32[]{:S(2)}) collective-permute-start(bf16[256,512]{1,0:T(8,128)(2,1)S(1)} %pad_maximum_fusion.4), channel_id=1, source_target_pairs={{0,3},{1,2},{2,1},{3,0},{4,7},{5,6},{6,5},{7,4},{8,11},{9,10},{10,... | collective-permute-start | bytes 786440 | tf_op jit(solution)/shard_map/ppermute | solution.py:63
  6.4 3.2 %pad_maximum_fusion = bf16[528,2048]{1,0:T(8,128)(2,1)} fusion(bf16[176,2048]{1,0:T(8,128)(2,1)} %bitcast.28, bf16[176,2048]{1,0:T(8,128)(2,1)} %bitcast.29, bf16[176,2048]{1,0:T(8,128)(2,1)} %bitcast.30), kind=kLoop, calls=%fused_computation.7 | loop fusion | flops 6488064 | bytes 4325376 | tf_op jit(solution)/shard_map/concatenate | solution.py:297
  9.6 3.3 %collective-permute-done.got_ref = bf16[256,512]{1,0:T(8,128)(2,1)S(1)} collective-permute-done((bf16[256,512]{1,0:T(8,128)(2,1)S(1)}, bf16[256,512]{1,0:T(8,128)(2,1)S(1)}, u32[]{:S(2)}, u32[]{:S(2)}) %collective-permute-start) | collective-permute-done | bytes 262176 | tf_op jit(solution)/shard_map/ppermute | solution.py:63
  12.9 4.7 %collective-permute-start.2 = (bf16[528,2048]{1,0:T(8,128)(2,1)}, bf16[528,2048]{1,0:T(8,128)(2,1)}, u32[]{:S(2)}, u32[]{:S(2)}) collective-permute-start(bf16[528,2048]{1,0:T(8,128)(2,1)} %pad_maximum_fusion), channel_id=1, source_target_pairs={{0,3},{1,2},{2,1},{3,0},{4,7},{5,6},{6,5},{7,4},{8,11},{9,10},{10,... | collective-permute-start | bytes 6488072 | tf_op jit(solution)/shard_map/ppermute | solution.py:63
  17.8 2.9 %shard_map.110 = bf16[512,1280]{1,0:T(8,128)(2,1)} custom-call(s32[128,4]{1,0:T(8,128)S(1)} %copy.15.ids_ref, bf16[128,4]{1,0:T(8,128)(2,1)S(1)} %copy.16.probs_ref, bf16[128,512]{1,0:T(8,128)(2,1)S(1)} %copy-done, bf16[128,512]{1,0:T(8,128)(2,1)S(1)} %copy-done.1, bf16[256,512]{1,0:T(8,128)(2,1)S(1)} %collective-permute-done.got_ref), custom_call_target="tpu_custom_call" | custom-call | tf_op jit(solution)/shard_map/pallas_call | solution.py:29
  20.7 16.4 %all-to-all-start = ((bf16[64,8,1280]{2,1,0:T(8,128)(2,1)}), bf16[64,8,1280]{2,1,0:T(8,128)(2,1)S(1)}, u32[]{:S(2)}, u32[]{:S(2)}) async-start(bf16[64,8,1280]{2,1,0:T(8,128)(2,1)} %bitcast.3), calls=%async_computation | async-start | bytes 2621440 | tf_op jit(solution)/shard_map/all_to_all | solution.py:46
  37.1 27.1 %collective-permute-done.2 = bf16[528,2048]{1,0:T(8,128)(2,1)} collective-permute-done((bf16[528,2048]{1,0:T(8,128)(2,1)}, bf16[528,2048]{1,0:T(8,128)(2,1)}, u32[]{:S(2)}, u32[]{:S(2)}) %collective-permute-start.2) | collective-permute-done | bytes 2162720 | tf_op jit(solution)/shard_map/ppermute | solution.py:63
  64.2 1.9 collective-permute-start.3
  66.1 5.0 %all-to-all-done = bf16[64,8,1280]{2,1,0:T(8,128)(2,1)S(1)} async-done(((bf16[64,8,1280]{2,1,0:T(8,128)(2,1)}), bf16[64,8,1280]{2,1,0:T(8,128)(2,1)S(1)}, u32[]{:S(2)}, u32[]{:S(2)}) %all-to-all-start) | async-done | bytes 1310752 | tf_op jit(solution)/shard_map/all_to_all | solution.py:46
  71.3 1.9 collective-permute-start.5
  73.2 1.9 collective-permute-start.4
  75.1 2.0 %slice_dynamic-update-slice_fusion.8 = bf16[1536,2048]{1,0:T(8,128)(2,1)} fusion(bf16[528,2048]{1,0:T(8,128)(2,1)} %collective-permute-done.2), kind=kLoop, calls=%fused_computation.21 | loop fusion | bytes 1441792
  77.2 4.1 %collective-permute-start.1 = (bf16[512,640]{1,0:T(8,128)(2,1)S(1)}, bf16[512,640]{1,0:T(8,128)(2,1)S(1)}, u32[]{:S(2)}, u32[]{:S(2)}) collective-permute-start(bf16[512,640]{1,0:T(8,128)(2,1)S(1)} %get-tuple-element.66.mine_ref), channel_id=1, source_target_pairs={{0,1},{1,0},{2,3},{3,2},{4,5},{5,4},{6,7},{7,6},{8,9},{9,8},{10,11... | collective-permute-start | bytes 1966088 | tf_op jit(solution)/shard_map/ppermute | solution.py:68
  81.3 9.6 %collective-permute-done.5.theirs_ref = bf16[512,640]{1,0:T(8,128)(2,1)S(1)} collective-permute-done((bf16[512,640]{1,0:T(8,128)(2,1)S(1)}, bf16[512,640]{1,0:T(8,128)(2,1)S(1)}, u32[]{:S(2)}, u32[]{:S(2)}) %collective-permute-start.5) | collective-permute-done | bytes 655392 | tf_op jit(solution)/shard_map/ppermute | solution.py:68
  92.0 2.1 %slice_dynamic-update-slice_fusion.7 = bf16[1536,2048]{1,0:T(8,128)(2,1)} fusion(bf16[1536,2048]{1,0:T(8,128)(2,1)} %slice_dynamic-update-slice_fusion.8, bf16[528,2048]{1,0:T(8,128)(2,1)} %collective-permute-done.3), kind=kLoop, calls=%fused_computation.20 | loop fusion | bytes 1441792
  94.8 2.4 %slice_dynamic-update-slice_fusion.2 = (bf16[768,2048]{1,0:T(8,128)(2,1)S(1)}, bf16[1536,2048]{1,0:T(8,128)(2,1)}) fusion(bf16[528,2048]{1,0:T(8,128)(2,1)} %collective-permute-done.2, bf16[1536,2048]{1,0:T(8,128)(2,1)} %broadcast_dynamic-update-slice_fusion.2), kind=kLoop, calls=%fused_computation.15 | loop fusion | bytes 2883584
  97.1 2.4 %slice_dynamic-update-slice_fusion.1 = (bf16[768,2048]{1,0:T(8,128)(2,1)S(1)}, bf16[1536,2048]{1,0:T(8,128)(2,1)}) fusion(bf16[768,2048]{1,0:T(8,128)(2,1)S(1)} %get-tuple-element.57, bf16[528,2048]{1,0:T(8,128)(2,1)} %collective-permute-done.3, bf16[1536,2048]{1,0:T(8,128)(2,1)} %get-tuple-element.58), kind=kLoop, calls=%fused_computation.14 | loop fusion | bytes 2883584
  100.1 2.1 %slice_dynamic-update-slice_fusion.11 = bf16[1536,2048]{1,0:T(8,128)(2,1)} fusion(bf16[1536,2048]{1,0:T(8,128)(2,1)} %get-tuple-element.67, bf16[528,2048]{1,0:T(8,128)(2,1)} %pad_maximum_fusion), kind=kLoop, calls=%fused_computation.24 | loop fusion | bytes 1441792
  103.8 2.4 %slice_dynamic-update-slice_fusion.9 = (bf16[768,2048]{1,0:T(8,128)(2,1)S(1)}, bf16[1536,2048]{1,0:T(8,128)(2,1)}) fusion(bf16[768,2048]{1,0:T(8,128)(2,1)S(1)} %get-tuple-element.68, bf16[528,2048]{1,0:T(8,128)(2,1)} %pad_maximum_fusion, bf16[1536,2048]{1,0:T(8,128)(2,1)} %broadcast_dynamic-update-slice_fusion), kind=kLoop, calls=%fused_computation.22 | loop fusion | bytes 2883584
  110.3 5.0 %fusion.9.pre_ref = f32[320,1536]{1,0:T(8,128)S(1)} fusion(bf16[320,2048]{1,0:T(8,128)(2,1)S(1)} %shard_map.111, bf16[1536,2048]{1,0:T(8,128)(2,1)} %broadcast_dynamic-update-slice_fusion.5), kind=kOutput, calls=%fused_computation.45 | convolution fusion | flops 2013265920 | bytes 9568256 | tf_op jit(solution)/shard_map/dot_general | solution.py:23
  116.1 5.0 %convolution_convert_fusion.4.block_ref = bf16[320,2048]{1,0:T(8,128)(2,1)S(1)} fusion(bf16[320,1536]{1,0:T(8,128)(2,1)S(1)} %get-tuple-element.28, bf16[1536,2048]{1,0:T(8,128)(2,1)} %broadcast_dynamic-update-slice_fusion.5), kind=kOutput, calls=%fused_computation.6 | convolution fusion | flops 2013921280 | bytes 8585216 | tf_op jit(solution)/shard_map/dot_general | solution.py:23
  121.4 1.8 convolution_convert_fusion.1
  124.8 1.9 collective-permute-start.7
  126.7 2.1 %collective-permute-start.6 = (bf16[336,1024]{1,0:T(8,128)(2,1)S(1)}, bf16[336,1024]{1,0:T(8,128)(2,1)S(1)}, u32[]{:S(2)}, u32[]{:S(2)}) collective-permute-start(bf16[336,1024]{1,0:T(8,128)(2,1)S(1)} %pad_maximum_fusion.3), channel_id=1, source_target_pairs={{0,1},{1,0},{2,3},{3,2},{4,5},{5,4},{6,7},{7,6},{8,9},{9,8},{10,11... | collective-permute-start | bytes 2064392 | tf_op jit(solution)/shard_map/ppermute | solution.py:68
  133.7 2.4 %collective-permute-start.9 = (bf16[528,2048]{1,0:T(8,128)(2,1)}, bf16[528,2048]{1,0:T(8,128)(2,1)}, u32[]{:S(2)}, u32[]{:S(2)}) collective-permute-start(bf16[528,2048]{1,0:T(8,128)(2,1)} %pad_maximum_fusion.2), channel_id=1, source_target_pairs={{0,4},{4,0},{8,12},{12,8},{16,20},{20,16},{24,28},{28,24},{32,36},... | collective-permute-start | bytes 6488072 | tf_op jit(solution)/shard_map/ppermute | solution.py:58
  136.2 2.4 %add_convert_fusion.1 = bf16[528,2048]{1,0:T(8,128)(2,1)} fusion(bf16[528,2048]{1,0:T(8,128)(2,1)S(1)} %collective-permute-done.7, bf16[176,2048]{1,0:T(8,128)(2,1)S(1)} %get-tuple-element.61, bf16[176,2048]{1,0:T(8,128)(2,1)S(1)} %get-tuple-element.47, bf16[176,2048]{1,0:T(8,128)(2,1)S(1)} %get-tuple-element.44), kind=kLoop, calls=%fused_computation.1 | loop fusion | flops 9732096 | bytes 6488064 | tf_op jit(solution)/shard_map/convert_element_type | solution.py:362
  138.5 2.4 %collective-permute-start.10 = (bf16[528,2048]{1,0:T(8,128)(2,1)}, bf16[528,2048]{1,0:T(8,128)(2,1)}, u32[]{:S(2)}, u32[]{:S(2)}) collective-permute-start(bf16[528,2048]{1,0:T(8,128)(2,1)} %add_convert_fusion.1), channel_id=1, source_target_pairs={{0,3},{1,2},{2,1},{3,0},{4,7},{5,6},{6,5},{7,4},{8,11},{9,10},{10,... | collective-permute-start | bytes 6488072 | tf_op jit(solution)/shard_map/ppermute | solution.py:63
  140.9 5.5 %collective-permute-done.6.got_ref = bf16[336,1024]{1,0:T(8,128)(2,1)S(1)} collective-permute-done((bf16[336,1024]{1,0:T(8,128)(2,1)S(1)}, bf16[336,1024]{1,0:T(8,128)(2,1)S(1)}, u32[]{:S(2)}, u32[]{:S(2)}) %collective-permute-start.6) | collective-permute-done | bytes 688160 | tf_op jit(solution)/shard_map/ppermute | solution.py:68
  147.4 35.2 %all_to_all.10 = bf16[64,8,768]{2,1,0:T(8,128)(2,1)S(1)} all-to-all(bf16[64,8,768]{2,1,0:T(8,128)(2,1)S(1)} %bitcast.27), channel_id=1, replica_groups={{0,8,16,24,32,40,48,56,64,72,80,88,96,104,112,120,128,136,144,152,160,1..., dimensions={0} | all-to-all | bytes 1572864 | tf_op jit(solution)/shard_map/all_to_all | solution.py:46
  183.6 4.7 %collective-permute-start.8 = (bf16[128,640]{1,0:T(8,128)(2,1)S(1)}, bf16[128,640]{1,0:T(8,128)(2,1)S(1)}, u32[]{:S(2)}, u32[]{:S(2)}) collective-permute-start(bf16[128,640]{1,0:T(8,128)(2,1)S(1)} %get-tuple-element.32.pass_ref), channel_id=1, source_target_pairs={{0,3},{1,2},{2,1},{3,0},{4,7},{5,6},{6,5},{7,4},{8,11},{9,10},{10,... | collective-permute-start | bytes 491528 | tf_op jit(solution)/shard_map/ppermute | solution.py:63
  188.3 6.0 %collective-permute-done.8.got_ref = bf16[128,640]{1,0:T(8,128)(2,1)S(1)} collective-permute-done((bf16[128,640]{1,0:T(8,128)(2,1)S(1)}, bf16[128,640]{1,0:T(8,128)(2,1)S(1)}, u32[]{:S(2)}, u32[]{:S(2)}) %collective-permute-start.8) | collective-permute-done | bytes 163872 | tf_op jit(solution)/shard_map/ppermute | solution.py:63
  196.0 3.6 %add_convert_fusion = bf16[528,2048]{1,0:T(8,128)(2,1)S(1)} fusion(bf16[528,2048]{1,0:T(8,128)(2,1)} %collective-permute-done.10, bf16[528,2048]{1,0:T(8,128)(2,1)} %collective-permute-done.9, bf16[176,2048]{1,0:T(8,128)(2,1)S(1)} %get-tuple-element.59, bf16[176,2048]{1,0:T(8,128)(2,1)S(1)} %get-tuple-element.43, bf16[176,2048]{1,0:T(8,128)(2,1)S(1)} %get-tuple-element.40), kind=kLoop, calls=%fused_computation | loop fusion | flops 11894784 | bytes 8650752 | tf_op jit(solution)/shard_map/convert_element_type | solution.py:365
  (46 shorter events, 22.2 us)
Async XLA Ops:
  0.6 17.2 %copy-start = (bf16[128,512]{1,0:T(8,128)(2,1)S(1)}, bf16[128,512]{1,0:T(8,128)(2,1)}, u32[]{:S(2)}) copy-start(bf16[128,512]{1,0:T(8,128)(2,1)} %own_x_ref.1) | copy-start | bytes 393220
  0.6 17.2 %copy-start.1 = (bf16[128,512]{1,0:T(8,128)(2,1)S(1)}, bf16[128,512]{1,0:T(8,128)(2,1)}, u32[]{:S(2)}) copy-start(bf16[128,512]{1,0:T(8,128)(2,1)} %own_dy_ref.1) | copy-start | bytes 393220
  0.7 16.9 %copy-start.2 = (s32[128,4]{0,1:T(4,128)S(1)}, s32[128,4]{0,1:T(4,128)}, u32[]{:S(2)}) copy-start(s32[128,4]{0,1:T(4,128)} %param.9) | copy-start | bytes 6148
  0.7 17.0 %copy-start.3 = (bf16[128,4]{0,1:T(4,128)(2,1)S(1)}, bf16[128,4]{0,1:T(4,128)(2,1)}, u32[]{:S(2)}) copy-start(bf16[128,4]{0,1:T(4,128)(2,1)} %param.10) | copy-start | bytes 3076
  1.7 11.2 %collective-permute-start = (bf16[256,512]{1,0:T(8,128)(2,1)S(1)}, bf16[256,512]{1,0:T(8,128)(2,1)S(1)}, u32[]{:S(2)}, u32[]{:S(2)}) collective-permute-start(bf16[256,512]{1,0:T(8,128)(2,1)S(1)} %pad_maximum_fusion.4), channel_id=1, source_target_pairs={{0,3},{1,2},{2,1},{3,0},{4,7},{5,6},{6,5},{7,4},{8,11},{9,10},{10,... | collective-permute-start | bytes 786440 | tf_op jit(solution)/shard_map/ppermute | solution.py:63
  12.9 51.3 %collective-permute-start.2 = (bf16[528,2048]{1,0:T(8,128)(2,1)}, bf16[528,2048]{1,0:T(8,128)(2,1)}, u32[]{:S(2)}, u32[]{:S(2)}) collective-permute-start(bf16[528,2048]{1,0:T(8,128)(2,1)} %pad_maximum_fusion), channel_id=1, source_target_pairs={{0,3},{1,2},{2,1},{3,0},{4,7},{5,6},{6,5},{7,4},{8,11},{9,10},{10,... | collective-permute-start | bytes 6488072 | tf_op jit(solution)/shard_map/ppermute | solution.py:63
  20.7 50.5 %all-to-all-start = ((bf16[64,8,1280]{2,1,0:T(8,128)(2,1)}), bf16[64,8,1280]{2,1,0:T(8,128)(2,1)S(1)}, u32[]{:S(2)}, u32[]{:S(2)}) async-start(bf16[64,8,1280]{2,1,0:T(8,128)(2,1)} %bitcast.3), calls=%async_computation | async-start | bytes 2621440 | tf_op jit(solution)/shard_map/all_to_all | solution.py:46
  64.2 27.8 %collective-permute-start.3 = (bf16[528,2048]{1,0:T(8,128)(2,1)}, bf16[528,2048]{1,0:T(8,128)(2,1)}, u32[]{:S(2)}, u32[]{:S(2)}) collective-permute-start(bf16[528,2048]{1,0:T(8,128)(2,1)} %collective-permute-done.2), channel_id=1, source_target_pairs={{0,4},{4,0},{8,12},{12,8},{16,20},{20,16},{24,28},{28,24},{32,36},... | collective-permute-start | bytes 6488072 | tf_op jit(solution)/shard_map/ppermute | solution.py:58
  71.3 19.6 %collective-permute-start.5 = (bf16[512,640]{1,0:T(8,128)(2,1)S(1)}, bf16[512,640]{1,0:T(8,128)(2,1)S(1)}, u32[]{:S(2)}, u32[]{:S(2)}) collective-permute-start(bf16[512,640]{1,0:T(8,128)(2,1)S(1)} %get-tuple-element.65.mine_ref), channel_id=1, source_target_pairs={{0,1},{1,0},{2,3},{3,2},{4,5},{5,4},{6,7},{7,6},{8,9},{9,8},{10,11... | collective-permute-start | bytes 1966088 | tf_op jit(solution)/shard_map/ppermute | solution.py:68
  73.2 29.0 %collective-permute-start.4 = (bf16[528,2048]{1,0:T(8,128)(2,1)}, bf16[528,2048]{1,0:T(8,128)(2,1)S(1)}, u32[]{:S(2)}, u32[]{:S(2)}) collective-permute-start(bf16[528,2048]{1,0:T(8,128)(2,1)} %pad_maximum_fusion), channel_id=1, source_target_pairs={{0,4},{4,0},{8,12},{12,8},{16,20},{20,16},{24,28},{28,24},{32,36},... | collective-permute-start | bytes 6488072 | tf_op jit(solution)/shard_map/ppermute | solution.py:58
  77.2 30.7 %collective-permute-start.1 = (bf16[512,640]{1,0:T(8,128)(2,1)S(1)}, bf16[512,640]{1,0:T(8,128)(2,1)S(1)}, u32[]{:S(2)}, u32[]{:S(2)}) collective-permute-start(bf16[512,640]{1,0:T(8,128)(2,1)S(1)} %get-tuple-element.66.mine_ref), channel_id=1, source_target_pairs={{0,1},{1,0},{2,3},{3,2},{4,5},{5,4},{6,7},{7,6},{8,9},{9,8},{10,11... | collective-permute-start | bytes 1966088 | tf_op jit(solution)/shard_map/ppermute | solution.py:68
  124.8 11.4 %collective-permute-start.7 = (bf16[528,2048]{1,0:T(8,128)(2,1)S(1)}, bf16[528,2048]{1,0:T(8,128)(2,1)S(1)}, u32[]{:S(2)}, u32[]{:S(2)}) collective-permute-start(bf16[528,2048]{1,0:T(8,128)(2,1)S(1)} %pad_maximum_fusion.1), channel_id=1, source_target_pairs={{0,4},{4,0},{8,12},{12,8},{16,20},{20,16},{24,28},{28,24},{32,36},... | collective-permute-start | bytes 6488072 | tf_op jit(solution)/shard_map/ppermute | solution.py:58
  126.7 19.7 %collective-permute-start.6 = (bf16[336,1024]{1,0:T(8,128)(2,1)S(1)}, bf16[336,1024]{1,0:T(8,128)(2,1)S(1)}, u32[]{:S(2)}, u32[]{:S(2)}) collective-permute-start(bf16[336,1024]{1,0:T(8,128)(2,1)S(1)} %pad_maximum_fusion.3), channel_id=1, source_target_pairs={{0,1},{1,0},{2,3},{3,2},{4,5},{5,4},{6,7},{7,6},{8,9},{9,8},{10,11... | collective-permute-start | bytes 2064392 | tf_op jit(solution)/shard_map/ppermute | solution.py:68
  133.7 62.3 %collective-permute-start.9 = (bf16[528,2048]{1,0:T(8,128)(2,1)}, bf16[528,2048]{1,0:T(8,128)(2,1)}, u32[]{:S(2)}, u32[]{:S(2)}) collective-permute-start(bf16[528,2048]{1,0:T(8,128)(2,1)} %pad_maximum_fusion.2), channel_id=1, source_target_pairs={{0,4},{4,0},{8,12},{12,8},{16,20},{20,16},{24,28},{28,24},{32,36},... | collective-permute-start | bytes 6488072 | tf_op jit(solution)/shard_map/ppermute | solution.py:58
  138.5 57.5 %collective-permute-start.10 = (bf16[528,2048]{1,0:T(8,128)(2,1)}, bf16[528,2048]{1,0:T(8,128)(2,1)}, u32[]{:S(2)}, u32[]{:S(2)}) collective-permute-start(bf16[528,2048]{1,0:T(8,128)(2,1)} %add_convert_fusion.1), channel_id=1, source_target_pairs={{0,3},{1,2},{2,1},{3,0},{4,7},{5,6},{6,5},{7,4},{8,11},{9,10},{10,... | collective-permute-start | bytes 6488072 | tf_op jit(solution)/shard_map/ppermute | solution.py:63
  183.6 10.7 %collective-permute-start.8 = (bf16[128,640]{1,0:T(8,128)(2,1)S(1)}, bf16[128,640]{1,0:T(8,128)(2,1)S(1)}, u32[]{:S(2)}, u32[]{:S(2)}) collective-permute-start(bf16[128,640]{1,0:T(8,128)(2,1)S(1)} %get-tuple-element.32.pass_ref), channel_id=1, source_target_pairs={{0,3},{1,2},{2,1},{3,0},{4,7},{5,6},{6,5},{7,4},{8,11},{9,10},{10,... | collective-permute-start | bytes 491528 | tf_op jit(solution)/shard_map/ppermute | solution.py:63

commit v3 on v2

--- a/solution.py
+++ b/solution.py
@@ -25,11 +25,13 @@
     )
 
 
-def local_call(body, out_shape, *operands):
+def local_call(body, out_shape, *operands, mib=12, **options):
     return pl.pallas_call(
         body,
         out_shape=out_shape,
-        compiler_params=pltpu.CompilerParams(vmem_limit_bytes=48 * 1024 * 1024),
+        cost_estimate=pl.CostEstimate(flops=0, bytes_accessed=0, transcendentals=0),
+        compiler_params=pltpu.CompilerParams(vmem_limit_bytes=mib * 1024 * 1024),
+        **options,
     )(*operands)
 
 
@@ -140,13 +142,11 @@
     )
 
 
-def unpack_kernel(mine_ref, theirs_ref, full_ref):
-    wide = mine_ref.shape[0]
+def unpack(mine, theirs, outer, full_ref):
+    wide = mine.shape[0]
     quarter = full_ref.shape[1] // 4
     experts = wide // TILE
     heads = experts * HEAD
-    outer = is_outer()
-    mine, theirs = mine_ref[...], theirs_ref[...]
     slot = iota(heads, wide, 0)
     source = iota(heads, wide, 1)
     rest_slot = iota(experts, wide, 0)
@@ -167,55 +167,124 @@
                 ).astype(bf16)
 
 
-def back_kernel(half, pre_ref, down_ref, joint_ref, hidden_ref, prob_ref):
-    slots = pre_ref.shape[0]
-    ones = jnp.ones((EXTRA, half), bf16)
-    total = jnp.zeros((EXTRA, slots), f32)
-    for part in range(2):
-        start = 2 * half * part
-        pre_gate = pre_ref[:, start : start + half]
-        pre_up = pre_ref[:, start + half : start + 2 * half]
-        down_back = down_ref[:, half * part : half * (part + 1)]
-        sigmoid = jax.nn.sigmoid(pre_gate)
-        silu_value = pre_gate * sigmoid
-        hidden = silu_value * pre_up
-        slope = sigmoid * (1.0 + pre_gate * (1.0 - sigmoid))
-        joint_ref[:, start : start + half] = (down_back * pre_up * slope).astype(bf16)
-        joint_ref[:, start + half : start + 2 * half] = (down_back * silu_value).astype(bf16)
-        hidden_ref[:, half * part : half * (part + 1)] = hidden.astype(bf16)
-        product = hidden * down_back
-        high = product.astype(bf16)
-        low = (product - high.astype(f32)).astype(bf16)
-        total += dot_f32(ones, high, 1, 1) + dot_f32(ones, low, 1, 1)
-    high = total.astype(bf16)
-    low = (total - high.astype(f32)).astype(bf16)
+def load_units(sources, kind, units, target, sems):
+    far, twin, own, own_twin = sources[0], sources[1 + kind], sources[4], sources[5]
+    rows = pl.ds(kind * units, units)
+    pieces = (far.at[rows], twin, own.at[rows], own_twin.at[rows])
+    copies = []
+    for place, piece in enumerate(pieces):
+        copy = pltpu.make_async_copy(
+            piece, target.at[pl.ds(place * units, units)], sems.at[kind * 4 + place]
+        )
+        copy.start()
+        copies.append(copy)
+    return copies
+
+
+def wait_all(copies):
+    for copy in copies:
+        copy.wait()
+
+
+def back_kernel(units, mine_ref, theirs_ref, *refs):
+    sources = refs[:6]
+    rows_ref, grads_ref, gate_ref, up_ref, sums_ref, given_ref = refs[6:12]
+    parts = refs[12:24]
+    w_gate, w_up, w_down, sems = refs[24:]
+    gate_copies = load_units(sources, 0, units, w_gate, sems)
+    up_copies = load_units(sources, 1, units, w_up, sems)
+    down_copies = load_units(sources, 2, units, w_down, sems)
+    outer = is_outer()
+    slots = rows_ref.shape[0]
+    edge = mine_ref.shape[1] // 2
+    unpack(mine_ref[:, :edge], theirs_ref[:, :edge], outer, rows_ref)
+    wait_all(gate_copies)
+    pre_gate = dot_f32(rows_ref[...], w_gate[...], 1, 1)
+    wait_all(up_copies)
+    pre_up = dot_f32(rows_ref[...], w_up[...], 1, 1)
+    unpack(mine_ref[:, edge:], theirs_ref[:, edge:], outer, grads_ref)
+    wait_all(down_copies)
+    down_back = dot_f32(grads_ref[...], w_down[...], 1, 1)
+    sigmoid = jax.nn.sigmoid(pre_gate)
+    silu_value = pre_gate * sigmoid
+    hidden = silu_value * pre_up
+    slope = sigmoid * (1.0 + pre_gate * (1.0 - sigmoid))
+    gate_back = (down_back * pre_up * slope).astype(bf16)
+    up_back = (down_back * silu_value).astype(bf16)
+    hidden_bf = hidden.astype(bf16)
+    gate_ref[...] = gate_back
+    up_ref[...] = up_back
+    for kind, value in enumerate((gate_back, up_back, hidden_bf)):
+        for place in range(4):
+            parts[3 * place + kind][...] = value[:, place * units : (place + 1) * units]
+    product = hidden * down_back
+    high = product.astype(bf16)
+    low = (product - high.astype(f32)).astype(bf16)
+    ones = jnp.ones((EXTRA, product.shape[1]), bf16)
+    total = dot_f32(ones, high, 1, 1) + dot_f32(ones, low, 1, 1)
+    high = total.astype(bf16).astype(f32)
     row = iota(EXTRA, slots, 0)
-    zero = jnp.zeros_like(high)
-    prob_ref[...] = jnp.zeros_like(prob_ref)
-    prob_ref[:, :slots] = jnp.where(row == 0, high, jnp.where(row == 1, low, zero))
-
-
-def give_kernel(block_ref, prob_ref, got_ref, give_ref):
-    slots = block_ref.shape[0]
-    quarter = block_ref.shape[1] // 4
+    sums = jnp.where(row == 0, high, jnp.where(row == 1, total - high, 0.0)).astype(bf16)
+    sums_ref[...] = jnp.zeros_like(sums_ref)
+    sums_ref[:, :slots] = sums
+    given_ref[slots:, :] = jnp.zeros((EXTRA, given_ref.shape[1]), bf16)
+    given_ref[slots:, :slots] = sums
+    blocks(gate_ref, up_ref, w_gate, w_up, outer, ((1, 0), (2, 3)), given_ref, slots)
+
+
+def blocks(gate_ref, up_ref, w_gate, w_up, outer, places, target, slots):
+    quarter = target.shape[1] // FOLDS
+    for fold, (outer_place, inner_place) in enumerate(places):
+        place = jnp.where(outer, outer_place, inner_place)
+        columns = pl.ds(pl.multiple_of(place * quarter, quarter), quarter)
+        block = dot_f32(gate_ref[...], w_gate[:, columns], 1, 0)
+        block += dot_f32(up_ref[...], w_up[:, columns], 1, 0)
+        target[:slots, fold * quarter : (fold + 1) * quarter] = block.astype(bf16)
+
+
+def keep_kernel(units, gate_ref, up_ref, sums_ref, *refs):
+    sources = refs[:6]
+    kept_ref, w_gate, w_up, sems = refs[6:]
+    gate_copies = load_units(sources, 0, units, w_gate, sems)
+    up_copies = load_units(sources, 1, units, w_up, sems)
+    slots = gate_ref.shape[0]
+    kept_ref[slots:] = sums_ref[...]
+    wait_all(gate_copies)
+    wait_all(up_copies)
+    blocks(gate_ref, up_ref, w_gate, w_up, is_outer(), ((0, 1), (3, 2)), kept_ref, slots)
+
+
+def grad_kernel(units, rows_ref, grads_ref, gate_ref, up_ref, hidden_ref, part_ref):
+    pairs = ((gate_ref, rows_ref), (up_ref, rows_ref), (hidden_ref, grads_ref))
+    for place, (back, source) in enumerate(pairs):
+        result = dot_f32(back[...], source[...], 0, 0)
+        part_ref[place * units : (place + 1) * units] = result.astype(bf16)
+
+
+def total_kernel(units, kept_ref, twin_ref, far_ref, gate_ref, up_ref, down_ref):
+    for place, target in enumerate((gate_ref, up_ref, down_ref)):
+        part = slice(place * units, (place + 1) * units)
+        target[...] = (
+            kept_ref[part].astype(f32) + twin_ref[part].astype(f32) + far_ref[part].astype(f32)
+        ).astype(bf16)
+
+
+def give_kernel(kept_ref, got_ref, give_ref):
+    slots = kept_ref.shape[0] - EXTRA
+    quarter = kept_ref.shape[1] // FOLDS
     wide = give_ref.shape[0]
     experts = wide // TILE
     heads = experts * HEAD
-    outer = is_outer()
     slot = iota(wide, heads, 1)
     target = iota(wide, heads, 0)
     rest_slot = iota(wide, experts, 1)
     rest_target = iota(wide, experts, 0)
     main = jnp.zeros((wide, quarter), f32)
     tail = jnp.zeros((wide, LANES), f32)
-    for fold, (outside, inside) in enumerate(((0, 1), (3, 2))):
-        kept = jnp.where(
-            outer,
-            block_ref[:, outside * quarter : (outside + 1) * quarter],
-            block_ref[:, inside * quarter : (inside + 1) * quarter],
-        )
-        got = got_ref[:slots, fold * quarter : (fold + 1) * quarter]
-        route = (kept.astype(f32) + got.astype(f32)).astype(bf16)
+    for fold in range(FOLDS):
+        columns = slice(fold * quarter, (fold + 1) * quarter)
+        route = kept_ref[:slots, columns].astype(f32) + got_ref[:slots, columns].astype(f32)
+        route = route.astype(bf16)
         pick = as_mask(target == slot // HEAD * TILE + fold * HEAD + slot % HEAD).astype(bf16)
         main += dot_f32(pick, route[:heads], 1, 0)
         for index in range(HEAD):
@@ -223,7 +292,7 @@
             tail += dot_f32(pick, route[heads:, index * LANES : (index + 1) * LANES], 1, 0)
     give_ref[:, :quarter] = main.astype(bf16)
     give_ref[:, quarter : quarter + LANES] = tail.astype(bf16)
-    both = prob_ref[:, :slots].astype(f32) + got_ref[slots:, :slots].astype(f32)
+    both = kept_ref[slots:, :slots].astype(f32) + got_ref[slots:, :slots].astype(f32)
     total = jnp.sum(both, axis=0, keepdims=True)
     high = total.astype(bf16).astype(f32)
     rows = iota(LANES, slots, 0)
@@ -277,11 +346,11 @@
     input_ref[...] = (own_ref[...] + got_ref[:, :quarter].astype(f32)).astype(bf16)
     total = pass_ref[:, quarter:].astype(f32) + got_ref[:, quarter:].astype(f32)
     expert = iota(tokens, LANES, 1) % (LANES // 2)
-    chosen = [
-        jnp.sum(jnp.where(ids[:, top : top + 1] == expert, total, 0.0), axis=1, keepdims=True)
-        for top in range(top_count)
-    ]
-    prob_ref[...] = jnp.concatenate(chosen, axis=1) / probs_ref[...].astype(f32)
+    ones = jnp.ones((TILE, LANES), bf16)
+    for top in range(top_count):
+        chosen = jnp.where(ids[:, top : top + 1] == expert, total, 0.0).astype(bf16)
+        sums = dot_f32(ones, chosen, 1, 1)[:1]
+        prob_ref[top : top + 1] = sums / probs_ref[top : top + 1].astype(f32)
 
 
 def shards(activations, cotangent, expert_ids, route_probs, gate_weight, up_weight, down_weight):
@@ -291,15 +360,12 @@
     wide = experts * TILE
     slots = experts * SHARE
     edge = quarter + LANES
-    outer = is_outer()
 
     got_tokens = row_partner(jnp.concatenate([activations, cotangent], axis=0))
     own_weights = jnp.concatenate([gate_weight[0], up_weight[0], down_weight[0]], axis=0)
     got_tokens, own_weights = lax.optimization_barrier((got_tokens, own_weights))
     far_weights = row_partner(own_weights)
     own_twin = other_core(own_weights)
-    far_twin = other_core(far_weights)
-
     send = local_call(
         pack_kernel,
         shape(wide, 2 * edge, bf16),
@@ -309,62 +375,63 @@
         cotangent,
         got_tokens,
     )
-    got = exchange_chips(send.reshape(experts, TILE, 2 * edge))
-    half = -(-2 * units // LANES) * LANES
-    gap = jnp.zeros((half - 2 * units, 4 * quarter), bf16)
-
-    def joined(index):
-        part = slice(index * units, (index + 1) * units)
-        return (
-            [far_weights[part], far_twin[part], gap],
-            [own_weights[part], own_twin[part], gap],
+    got = exchange_chips(send.reshape(experts, TILE, 2 * edge)).reshape(wide, 2 * edge)
+    theirs = unit_partner(got)
+    far_twin = [other_core(far_weights[i * units : (i + 1) * units]) for i in range(3)]
+    sources = (far_weights, *far_twin, own_weights, own_twin)
+
+    vmem = pl.BlockSpec(memory_space=pltpu.VMEM)
+    stay = pl.BlockSpec(memory_space=pl.ANY)
+    model = 4 * quarter
+    unit_rows = pltpu.VMEM((4 * units, model), bf16)
+    full = shape(slots, model, bf16)
+    back = shape(slots, 4 * units, bf16)
+    part = shape(slots, units, bf16)
+    full_rows, full_grads, gate_back, up_back, sums, given, *parts = local_call(
+        functools.partial(back_kernel, units),
+        (full, full, back, back)
+        + (shape(EXTRA, 2 * quarter, bf16), shape(slots + EXTRA, 2 * quarter, bf16))
+        + (part,) * 12,
+        got,
+        theirs,
+        *sources,
+        mib=30,
+        in_specs=[vmem] * 2 + [stay] * 6,
+        out_specs=(vmem,) * 18,
+        scratch_shapes=[unit_rows] * 3 + [pltpu.SemaphoreType.DMA((12,))],
+    )
+    taken = unit_partner(given)
+
+    def set_grads(place):
+        return local_call(
+            functools.partial(grad_kernel, units),
+            shape(3 * units, model, bf16),
+            full_rows,
+            full_grads,
+            *parts[3 * place : 3 * place + 3],
+            mib=16,
         )
 
-    (far_gate, own_gate), (far_up, own_up), (far_down, own_down) = joined(0), joined(1), joined(2)
-    wide_all = jnp.concatenate(far_gate + far_up + own_gate + own_up, axis=0)
-    down_all = jnp.concatenate(far_down + own_down, axis=0)
-    rows = got[:, :, :edge].reshape(wide, edge)
-    grads = got[:, :, edge:].reshape(wide, edge)
-    full = shape(slots, 4 * quarter, bf16)
-    their_rows = unit_partner(rows)
-    their_grads = unit_partner(grads)
-    their_rows, wide_all, down_all = lax.optimization_barrier((their_rows, wide_all, down_all))
-    full_rows = local_call(unpack_kernel, full, rows, their_rows)
-    full_grads = local_call(unpack_kernel, full, grads, their_grads)
-    pre = dot_f32(full_rows, wide_all, 1, 1)
-    down_back = dot_f32(full_grads, down_all, 1, 1)
-    joint, hidden, prob = local_call(
-        functools.partial(back_kernel, half),
-        (
-            shape(slots, 4 * half, bf16),
-            shape(slots, 2 * half, bf16),
-            shape(EXTRA, 2 * quarter, bf16),
-        ),
-        pre,
-        down_back,
-    )
-    block = dot_f32(joint, wide_all, 1, 0).astype(bf16)
-    outside = jnp.concatenate([block[:, :quarter], block[:, 3 * quarter :]], axis=1)
-    inside = block[:, quarter : 3 * quarter]
-    given = jnp.concatenate([jnp.where(outer, inside, outside), prob], axis=0)
-    taken = unit_partner(given)
-    given, joint_late, hidden_late = lax.optimization_barrier((given, joint, hidden))
-
-    def unit_grads(part):
-        wide_part = dot_f32(joint_late[:, 2 * half * part : 2 * half * (part + 1)], full_rows, 0, 0)
-        down_part = dot_f32(hidden_late[:, half * part : half * (part + 1)], full_grads, 0, 0)
-        wide_part, down_part = wide_part.astype(bf16), down_part.astype(bf16)
-        starts = ((wide_part, 0), (wide_part, half), (down_part, 0))
-        kept = jnp.concatenate([a[s : s + units] for a, s in starts], axis=0)
-        sent = jnp.concatenate([a[s + units : s + 2 * units] for a, s in starts], axis=0)
-        return kept.astype(f32) + other_core(sent).astype(f32)
-
-    far_grads = unit_grads(0).astype(bf16)
+    far_taken = other_core(set_grads(1))
+    far_grads = (set_grads(0).astype(f32) + far_taken.astype(f32)).astype(bf16)
     far_got = row_partner(far_grads)
+    near_taken = other_core(set_grads(3))
+    near_kept = set_grads(2)
+    kept = local_call(
+        functools.partial(keep_kernel, units),
+        shape(slots + EXTRA, 2 * quarter, bf16),
+        gate_back,
+        up_back,
+        sums,
+        *sources,
+        mib=18,
+        in_specs=[vmem] * 3 + [stay] * 6,
+        out_specs=vmem,
+        scratch_shapes=[unit_rows] * 2 + [pltpu.SemaphoreType.DMA((12,))],
+    )
     taken, far_grads = lax.optimization_barrier((taken, far_grads))
-    own_grads = (unit_grads(1) + far_got.astype(f32)).astype(bf16)
-
-    give = local_call(give_kernel, shape(wide, edge + LANES, bf16), block, prob, taken)
+
+    give = local_call(give_kernel, shape(wide, edge + LANES, bf16), kept, taken)
     back = exchange_chips(give.reshape(experts, TILE, edge + LANES)).reshape(wide, edge + LANES)
     own_sum, passed = local_call(
         combine_kernel,
@@ -372,22 +439,33 @@
         expert_ids,
         back,
     )
+    got_passed = row_partner(passed)
+    unit_grad = shape(units, model, bf16)
+    whole = pl.BlockSpec((3 * units, quarter), lambda i: (0, i))
+    third = pl.BlockSpec((units, quarter), lambda i: (0, i))
+    gate_grad, up_grad, down_grad = local_call(
+        functools.partial(total_kernel, units),
+        (unit_grad,) * 3,
+        near_kept,
+        near_taken,
+        far_got,
+        grid=(4,),
+        in_specs=[whole] * 3,
+        out_specs=(third,) * 3,
+    )
+    got_passed, gate_grad, up_grad, down_grad = lax.optimization_barrier(
+        (got_passed, gate_grad, up_grad, down_grad)
+    )
     input_grad, prob_grad = local_call(
         finish_kernel,
-        (shape(tokens, quarter, bf16), shape(tokens, expert_ids.shape[1], f32)),
+        (shape(tokens, quarter, bf16), shape(expert_ids.shape[1], tokens, f32)),
         expert_ids,
-        route_probs,
+        route_probs.T,
         own_sum,
         passed,
-        row_partner(passed),
-    )
-    return (
-        input_grad,
-        prob_grad,
-        own_grads[:units][None],
-        own_grads[units : 2 * units][None],
-        own_grads[2 * units :][None],
-    )
+        got_passed,
+    )
+    return (input_grad, prob_grad.T, gate_grad[None], up_grad[None], down_grad[None])
 
 
 def solution(mesh):

time: 202 us -> 176 us (0.87)
  the two profiles are of different devices: /device:TPU:24 before, /device:TPU:16 now
where the time goes in v3:
time: 176 us; the launch traced here: 175 us
  waiting for transfers between devices  52.9 us (30%)
  starting transfers between devices  51.9 us (29%)
  blocking collectives  34.9 us (20%)
  Pallas kernels  27.7 us (16%)
  other arithmetic  3.52 us (2%)
  local copies, waits for them, and re-layouts  3.4 us (2%)
    all_to_all x1, blocking collectives, exchange_chips(): lax.all_to_all(block, 'ep', split_axis=0, concat_axis=0, axis_index_group...  34.9 us
    all_to_all x1, waiting for transfers between devices, exchange_chips(): lax.all_to_all(block, 'ep', split_axis=0, concat_axis=0, axis_index_group...  28.4 us
    pallas_call x11, Pallas kernels, local_call(): pl.pallas_call(body, out_shape=out_shape, cost_estimate=pl.CostEstimate(f...  27.7 us
    ppermute x4, starting transfers between devices, row_partner(): lax.ppermute(value, 'et', [(source, count - 1 - source) for source in ran...  18.7 us
    ppermute x4, waiting for transfers between devices, row_partner(): lax.ppermute(value, 'et', [(source, count - 1 - source) for source in ran...  16.5 us
    all_to_all x1, starting transfers between devices, exchange_chips(): lax.all_to_all(block, 'ep', split_axis=0, concat_axis=0, axis_index_group...  16.5 us
    ppermute x6, starting transfers between devices, other_core(): return lax.ppermute(value, 'ep', pairs)  12.4 us
    ppermute x2, waiting for transfers between devices, unit_partner(): return lax.ppermute(value, 'et', pairs)  5.86 us
  transfers between devices with their start and end apart: 13, of which 6 were waited for; matrix products, arithmetic and copies ran while one was open for 3% of the time, Pallas kernels for 7%

profile of v3, /device:TPU:16, one launch (start us, length us, event | category | flops | bytes accessed | tf_op | source)
XLA Modules:
  0.0 175.3 jit_solution(17146704016401560992)
XLA Ops:
  0.6 1.0 pad_maximum_fusion.1
  1.6 4.7 %collective-permute-start = (bf16[256,512]{1,0:T(8,128)(2,1)S(1)}, bf16[256,512]{1,0:T(8,128)(2,1)S(1)}, u32[]{:S(2)}, u32[]{:S(2)}) collective-permute-start(bf16[256,512]{1,0:T(8,128)(2,1)S(1)} %pad_maximum_fusion.1), channel_id=1, source_target_pairs={{0,3},{1,2},{2,1},{3,0},{4,7},{5,6},{6,5},{7,4},{8,11},{9,10},{10,... | collective-permute-start | bytes 786440 | tf_op jit(solution)/shard_map/ppermute | solution.py:65
  7.9 1.7 pad_maximum_fusion.refs_4_
  9.6 3.1 %collective-permute-done.got_ref = bf16[256,512]{1,0:T(8,128)(2,1)S(1)} collective-permute-done((bf16[256,512]{1,0:T(8,128)(2,1)S(1)}, bf16[256,512]{1,0:T(8,128)(2,1)S(1)}, u32[]{:S(2)}, u32[]{:S(2)}) %collective-permute-start) | collective-permute-done | bytes 262176 | tf_op jit(solution)/shard_map/ppermute | solution.py:65
  12.8 2.9 %shard_map.110 = bf16[512,1280]{1,0:T(8,128)(2,1)} custom-call(s32[128,4]{1,0:T(8,128)S(1)} %copy.15.ids_ref, bf16[128,4]{1,0:T(8,128)(2,1)S(1)} %copy.13.probs_ref, bf16[128,512]{1,0:T(8,128)(2,1)S(1)} %copy-done, bf16[128,512]{1,0:T(8,128)(2,1)S(1)} %copy-done.1, bf16[256,512]{1,0:T(8,128)(2,1)S(1)} %collective-permute-done.got_ref), custom_call_target="tpu_custom_call" | custom-call | tf_op jit(solution)/shard_map/pallas_call | solution.py:29
  15.6 16.5 %all-to-all-start = ((bf16[64,8,1280]{2,1,0:T(8,128)(2,1)}), bf16[64,8,1280]{2,1,0:T(8,128)(2,1)S(1)}, u32[]{:S(2)}, u32[]{:S(2)}) async-start(bf16[64,8,1280]{2,1,0:T(8,128)(2,1)} %bitcast.4), calls=%async_computation | async-start | bytes 2621440 | tf_op jit(solution)/shard_map/all_to_all | solution.py:48
  32.1 4.7 %collective-permute-start.2 = (bf16[528,2048]{1,0:T(8,128)(2,1)S(1)}, bf16[528,2048]{1,0:T(8,128)(2,1)}, u32[]{:S(2)}, u32[]{:S(2)}) collective-permute-start(bf16[528,2048]{1,0:T(8,128)(2,1)S(1)} %pad_maximum_fusion.refs_4_), channel_id=1, source_target_pairs={{0,3},{1,2},{2,1},{3,0},{4,7},{5,6},{6,5},{7,4},{8,11},{9,10},{10,... | collective-permute-start | bytes 6488072 | tf_op jit(solution)/shard_map/ppermute | solution.py:65
  36.8 1.9 %collective-permute-start.6 = (bf16[528,2048]{1,0:T(8,128)(2,1)S(1)}, bf16[528,2048]{1,0:T(8,128)(2,1)}, u32[]{:S(2)}, u32[]{:S(2)}) collective-permute-start(bf16[528,2048]{1,0:T(8,128)(2,1)S(1)} %pad_maximum_fusion.refs_4_), channel_id=1, source_target_pairs={{0,4},{4,0},{8,12},{12,8},{16,20},{20,16},{24,28},{28,24},{32,36},... | collective-permute-start | bytes 6488072 | tf_op jit(solution)/shard_map/ppermute | solution.py:60
  38.7 28.4 %all-to-all-done = bf16[64,8,1280]{2,1,0:T(8,128)(2,1)S(1)} async-done(((bf16[64,8,1280]{2,1,0:T(8,128)(2,1)}), bf16[64,8,1280]{2,1,0:T(8,128)(2,1)S(1)}, u32[]{:S(2)}, u32[]{:S(2)}) %all-to-all-start) | async-done | bytes 1310752 | tf_op jit(solution)/shard_map/all_to_all | solution.py:48
  67.1 2.2 %collective-permute-start.1 = (bf16[512,1280]{1,0:T(8,128)(2,1)S(1)}, bf16[512,1280]{1,0:T(8,128)(2,1)S(1)}, u32[]{:S(2)}, u32[]{:S(2)}) collective-permute-start(bf16[512,1280]{1,0:T(8,128)(2,1)S(1)} %bitcast.12), channel_id=1, source_target_pairs={{0,1},{1,0},{2,3},{3,2},{4,5},{5,4},{6,7},{7,6},{8,9},{9,8},{10,11... | collective-permute-start | bytes 3932168 | tf_op jit(solution)/shard_map/ppermute | solution.py:70
  69.3 13.4 %collective-permute-done.2.refs_0_ = bf16[528,2048]{1,0:T(8,128)(2,1)} collective-permute-done((bf16[528,2048]{1,0:T(8,128)(2,1)S(1)}, bf16[528,2048]{1,0:T(8,128)(2,1)}, u32[]{:S(2)}, u32[]{:S(2)}) %collective-permute-start.2) | collective-permute-done | bytes 2162720 | tf_op jit(solution)/shard_map/ppermute | solution.py:65
  82.7 1.8 %fusion = (bf16[176,2048]{1,0:T(8,128)(2,1)S(1)}, bf16[176,2048]{1,0:T(8,128)(2,1)S(1)}, bf16[176,2048]{1,0:T(8,128)(2,1)S(1)}) fusion(bf16[528,2048]{1,0:T(8,128)(2,1)} %collective-permute-done.2.refs_0_), kind=kLoop, calls=%fused_computation.3 | loop fusion | bytes 4325376 | tf_op jit(solution)/shard_map/slice | solution.py:380
  84.5 1.9 %collective-permute-start.5 = (bf16[176,2048]{1,0:T(8,128)(2,1)S(1)}, bf16[176,2048]{1,0:T(8,128)(2,1)S(1)}, u32[]{:S(2)}, u32[]{:S(2)}) collective-permute-start(bf16[176,2048]{1,0:T(8,128)(2,1)S(1)} %get-tuple-element.69), channel_id=1, source_target_pairs={{0,4},{4,0},{8,12},{12,8},{16,20},{20,16},{24,28},{28,24},{32,36},... | collective-permute-start | bytes 2162696 | tf_op jit(solution)/shard_map/ppermute | solution.py:60
  86.4 2.4 %collective-permute-start.4 = (bf16[176,2048]{1,0:T(8,128)(2,1)S(1)}, bf16[176,2048]{1,0:T(8,128)(2,1)S(1)}, u32[]{:S(2)}, u32[]{:S(2)}) collective-permute-start(bf16[176,2048]{1,0:T(8,128)(2,1)S(1)} %get-tuple-element.70), channel_id=1, source_target_pairs={{0,4},{4,0},{8,12},{12,8},{16,20},{20,16},{24,28},{28,24},{32,36},... | collective-permute-start | bytes 2162696 | tf_op jit(solution)/shard_map/ppermute | solution.py:60
  88.8 1.9 %collective-permute-start.3 = (bf16[176,2048]{1,0:T(8,128)(2,1)S(1)}, bf16[176,2048]{1,0:T(8,128)(2,1)S(1)}, u32[]{:S(2)}, u32[]{:S(2)}) collective-permute-start(bf16[176,2048]{1,0:T(8,128)(2,1)S(1)} %get-tuple-element.71), channel_id=1, source_target_pairs={{0,4},{4,0},{8,12},{12,8},{16,20},{20,16},{24,28},{28,24},{32,36},... | collective-permute-start | bytes 2162696 | tf_op jit(solution)/shard_map/ppermute | solution.py:60
  90.8 2.1 %collective-permute-done.3.refs_1_ = bf16[176,2048]{1,0:T(8,128)(2,1)S(1)} collective-permute-done((bf16[176,2048]{1,0:T(8,128)(2,1)S(1)}, bf16[176,2048]{1,0:T(8,128)(2,1)S(1)}, u32[]{:S(2)}, u32[]{:S(2)}) %collective-permute-start.3) | collective-permute-done | bytes 720928 | tf_op jit(solution)/shard_map/ppermute | solution.py:60
  92.9 2.3 %collective-permute-done.1.theirs_ref = bf16[512,1280]{1,0:T(8,128)(2,1)S(1)} collective-permute-done((bf16[512,1280]{1,0:T(8,128)(2,1)S(1)}, bf16[512,1280]{1,0:T(8,128)(2,1)S(1)}, u32[]{:S(2)}, u32[]{:S(2)}) %collective-permute-start.1) | collective-permute-done | bytes 1310752 | tf_op jit(solution)/shard_map/ppermute | solution.py:70
  95.2 10.6 %shard_map.111 = (bf16[320,2048]{1,0:T(8,128)(2,1)S(1)}, bf16[320,2048]{1,0:T(8,128)(2,1)S(1)}, bf16[320,704]{1,0:T(8,128)(2,1)S(1)}, bf16[320,704]{1,0:T(8,128)...) custom-call(bf16[512,1280]{1,0:T(8,128)(2,1)S(1)} %bitcast.13, ...), custom_call_target="tpu_custom_call" | custom-call | tf_op jit(solution)/shard_map/pallas_call | solution.py:29
  105.8 1.3 shard_map.114
  107.1 2.1 %collective-permute-start.8 = (bf16[528,2048]{1,0:T(8,128)(2,1)S(1)}, bf16[528,2048]{1,0:T(8,128)(2,1)S(1)}, u32[]{:S(2)}, u32[]{:S(2)}) collective-permute-start(bf16[528,2048]{1,0:T(8,128)(2,1)S(1)} %shard_map.114), channel_id=1, source_target_pairs={{0,4},{4,0},{8,12},{12,8},{16,20},{20,16},{24,28},{28,24},{32,36},... | collective-permute-start | bytes 6488072 | tf_op jit(solution)/shard_map/ppermute | solution.py:60
  109.2 2.2 %collective-permute-start.7 = (bf16[336,1024]{1,0:T(8,128)(2,1)S(1)}, bf16[336,1024]{1,0:T(8,128)(2,1)S(1)}, u32[]{:S(2)}, u32[]{:S(2)}) collective-permute-start(bf16[336,1024]{1,0:T(8,128)(2,1)S(1)} %get-tuple-element.42), channel_id=1, source_target_pairs={{0,1},{1,0},{2,3},{3,2},{4,5},{5,4},{6,7},{7,6},{8,9},{9,8},{10,11... | collective-permute-start | bytes 2064392 | tf_op jit(solution)/shard_map/ppermute | solution.py:70
  111.4 1.3 shard_map.118
  112.7 2.1 %collective-permute-start.10 = (bf16[528,2048]{1,0:T(8,128)(2,1)S(1)}, bf16[528,2048]{1,0:T(8,128)(2,1)S(1)}, u32[]{:S(2)}, u32[]{:S(2)}) collective-permute-start(bf16[528,2048]{1,0:T(8,128)(2,1)S(1)} %shard_map.118), channel_id=1, source_target_pairs={{0,4},{4,0},{8,12},{12,8},{16,20},{20,16},{24,28},{28,24},{32,36},... | collective-permute-start | bytes 6488072 | tf_op jit(solution)/shard_map/ppermute | solution.py:60
  114.9 1.3 shard_map.113
  117.0 4.7 %collective-permute-start.11 = (bf16[528,2048]{1,0:T(8,128)(2,1)S(1)}, bf16[528,2048]{1,0:T(8,128)(2,1)S(1)}, u32[]{:S(2)}, u32[]{:S(2)}) collective-permute-start(bf16[528,2048]{1,0:T(8,128)(2,1)S(1)} %add_convert_fusion), channel_id=1, source_target_pairs={{0,3},{1,2},{2,1},{3,0},{4,7},{5,6},{6,5},{7,4},{8,11},{9,10},{10,... | collective-permute-start | bytes 6488072 | tf_op jit(solution)/shard_map/ppermute | solution.py:65
  121.7 3.7 %shard_map.112.kept_ref = bf16[336,1024]{1,0:T(8,128)(2,1)S(1)} custom-call(bf16[320,704]{1,0:T(8,128)(2,1)S(1)} %get-tuple-element.39.gate_ref, bf16[320,704]{1,0:T(8,128)(2,1)S(1)} %get-tuple-element.40.up_ref, bf16[16,1024]{1,0:T(8,128)(2,1)S(1)} %get-tuple-element.41.sums_ref, bf16[528,2048]{1,0:T(8,128)(2,1)} %collective-permute-done.2.refs_0_, ...), custom_call_target="tpu_custom_call" | custom-call | tf_op jit(solution)/shard_map/pallas_call | solution.py:29
  125.4 3.6 %collective-permute-done.7.got_ref = bf16[336,1024]{1,0:T(8,128)(2,1)S(1)} collective-permute-done((bf16[336,1024]{1,0:T(8,128)(2,1)S(1)}, bf16[336,1024]{1,0:T(8,128)(2,1)S(1)}, u32[]{:S(2)}, u32[]{:S(2)}) %collective-permute-start.7) | collective-permute-done | bytes 688160 | tf_op jit(solution)/shard_map/ppermute | solution.py:70
  129.9 34.9 %all_to_all.10 = bf16[64,8,768]{2,1,0:T(8,128)(2,1)S(1)} all-to-all(bf16[64,8,768]{2,1,0:T(8,128)(2,1)S(1)} %bitcast.15), channel_id=1, replica_groups={{0,8,16,24,32,40,48,56,64,72,80,88,96,104,112,120,128,136,144,152,160,1..., dimensions={0} | all-to-all | bytes 1572864 | tf_op jit(solution)/shard_map/all_to_all | solution.py:48
  164.8 1.0 shard_map.116
  165.9 4.7 %collective-permute-start.9 = (bf16[128,640]{1,0:T(8,128)(2,1)S(1)}, bf16[128,640]{1,0:T(8,128)(2,1)S(1)}, u32[]{:S(2)}, u32[]{:S(2)}) collective-permute-start(bf16[128,640]{1,0:T(8,128)(2,1)S(1)} %get-tuple-element.53.pass_ref), channel_id=1, source_target_pairs={{0,3},{1,2},{2,1},{3,0},{4,7},{5,6},{6,5},{7,4},{8,11},{9,10},{10,... | collective-permute-start | bytes 491528 | tf_op jit(solution)/shard_map/ppermute | solution.py:65
  170.5 1.3 shard_map.117.kept_ref
  171.9 2.5 %shard_map.119 = (bf16[176,2048]{1,0:T(8,128)(2,1)}, bf16[176,2048]{1,0:T(8,128)(2,1)}, bf16[176,2048]{1,0:T(8,128)(2,1)}) custom-call(bf16[528,2048]{1,0:T(8,128)(2,1)S(1)} %shard_map.117.kept_ref, bf16[528,2048]{1,0:T(8,128)(2,1)S(1)} %collective-permute-done.10.twin_ref, bf16[528,2048]{1,0:T(8,128)(2,1)S(1)} %collective-permute-done.11.far_ref), custom_call_target="tpu_custom_call" | custom-call | tf_op jit(solution)/shard_map/pallas_call | solution.py:29
  (18 shorter events, 4.3 us)
Async XLA Ops:
  1.6 11.2 %collective-permute-start = (bf16[256,512]{1,0:T(8,128)(2,1)S(1)}, bf16[256,512]{1,0:T(8,128)(2,1)S(1)}, u32[]{:S(2)}, u32[]{:S(2)}) collective-permute-start(bf16[256,512]{1,0:T(8,128)(2,1)S(1)} %pad_maximum_fusion.1), channel_id=1, source_target_pairs={{0,3},{1,2},{2,1},{3,0},{4,7},{5,6},{6,5},{7,4},{8,11},{9,10},{10,... | collective-permute-start | bytes 786440 | tf_op jit(solution)/shard_map/ppermute | solution.py:65
  7.9 4.9 %copy-start = (bf16[128,512]{1,0:T(8,128)(2,1)S(1)}, bf16[128,512]{1,0:T(8,128)(2,1)}, u32[]{:S(2)}) copy-start(bf16[128,512]{1,0:T(8,128)(2,1)} %own_x_ref.1) | copy-start | bytes 393220
  7.9 4.9 %copy-start.1 = (bf16[128,512]{1,0:T(8,128)(2,1)S(1)}, bf16[128,512]{1,0:T(8,128)(2,1)}, u32[]{:S(2)}) copy-start(bf16[128,512]{1,0:T(8,128)(2,1)} %own_dy_ref.1) | copy-start | bytes 393220
  15.6 51.4 %all-to-all-start = ((bf16[64,8,1280]{2,1,0:T(8,128)(2,1)}), bf16[64,8,1280]{2,1,0:T(8,128)(2,1)S(1)}, u32[]{:S(2)}, u32[]{:S(2)}) async-start(bf16[64,8,1280]{2,1,0:T(8,128)(2,1)} %bitcast.4), calls=%async_computation | async-start | bytes 2621440 | tf_op jit(solution)/shard_map/all_to_all | solution.py:48
  32.1 50.6 %collective-permute-start.2 = (bf16[528,2048]{1,0:T(8,128)(2,1)S(1)}, bf16[528,2048]{1,0:T(8,128)(2,1)}, u32[]{:S(2)}, u32[]{:S(2)}) collective-permute-start(bf16[528,2048]{1,0:T(8,128)(2,1)S(1)} %pad_maximum_fusion.refs_4_), channel_id=1, source_target_pairs={{0,3},{1,2},{2,1},{3,0},{4,7},{5,6},{6,5},{7,4},{8,11},{9,10},{10,... | collective-permute-start | bytes 6488072 | tf_op jit(solution)/shard_map/ppermute | solution.py:65
  36.8 53.9 %collective-permute-start.6 = (bf16[528,2048]{1,0:T(8,128)(2,1)S(1)}, bf16[528,2048]{1,0:T(8,128)(2,1)}, u32[]{:S(2)}, u32[]{:S(2)}) collective-permute-start(bf16[528,2048]{1,0:T(8,128)(2,1)S(1)} %pad_maximum_fusion.refs_4_), channel_id=1, source_target_pairs={{0,4},{4,0},{8,12},{12,8},{16,20},{20,16},{24,28},{28,24},{32,36},... | collective-permute-start | bytes 6488072 | tf_op jit(solution)/shard_map/ppermute | solution.py:60
  67.1 28.1 %collective-permute-start.1 = (bf16[512,1280]{1,0:T(8,128)(2,1)S(1)}, bf16[512,1280]{1,0:T(8,128)(2,1)S(1)}, u32[]{:S(2)}, u32[]{:S(2)}) collective-permute-start(bf16[512,1280]{1,0:T(8,128)(2,1)S(1)} %bitcast.12), channel_id=1, source_target_pairs={{0,1},{1,0},{2,3},{3,2},{4,5},{5,4},{6,7},{7,6},{8,9},{9,8},{10,11... | collective-permute-start | bytes 3932168 | tf_op jit(solution)/shard_map/ppermute | solution.py:70
  84.5 6.3 %collective-permute-start.5 = (bf16[176,2048]{1,0:T(8,128)(2,1)S(1)}, bf16[176,2048]{1,0:T(8,128)(2,1)S(1)}, u32[]{:S(2)}, u32[]{:S(2)}) collective-permute-start(bf16[176,2048]{1,0:T(8,128)(2,1)S(1)} %get-tuple-element.69), channel_id=1, source_target_pairs={{0,4},{4,0},{8,12},{12,8},{16,20},{20,16},{24,28},{28,24},{32,36},... | collective-permute-start | bytes 2162696 | tf_op jit(solution)/shard_map/ppermute | solution.py:60
  86.4 4.4 %collective-permute-start.4 = (bf16[176,2048]{1,0:T(8,128)(2,1)S(1)}, bf16[176,2048]{1,0:T(8,128)(2,1)S(1)}, u32[]{:S(2)}, u32[]{:S(2)}) collective-permute-start(bf16[176,2048]{1,0:T(8,128)(2,1)S(1)} %get-tuple-element.70), channel_id=1, source_target_pairs={{0,4},{4,0},{8,12},{12,8},{16,20},{20,16},{24,28},{28,24},{32,36},... | collective-permute-start | bytes 2162696 | tf_op jit(solution)/shard_map/ppermute | solution.py:60
  88.8 4.1 %collective-permute-start.3 = (bf16[176,2048]{1,0:T(8,128)(2,1)S(1)}, bf16[176,2048]{1,0:T(8,128)(2,1)S(1)}, u32[]{:S(2)}, u32[]{:S(2)}) collective-permute-start(bf16[176,2048]{1,0:T(8,128)(2,1)S(1)} %get-tuple-element.71), channel_id=1, source_target_pairs={{0,4},{4,0},{8,12},{12,8},{16,20},{20,16},{24,28},{28,24},{32,36},... | collective-permute-start | bytes 2162696 | tf_op jit(solution)/shard_map/ppermute | solution.py:60
  107.1 9.1 %collective-permute-start.8 = (bf16[528,2048]{1,0:T(8,128)(2,1)S(1)}, bf16[528,2048]{1,0:T(8,128)(2,1)S(1)}, u32[]{:S(2)}, u32[]{:S(2)}) collective-permute-start(bf16[528,2048]{1,0:T(8,128)(2,1)S(1)} %shard_map.114), channel_id=1, source_target_pairs={{0,4},{4,0},{8,12},{12,8},{16,20},{20,16},{24,28},{28,24},{32,36},... | collective-permute-start | bytes 6488072 | tf_op jit(solution)/shard_map/ppermute | solution.py:60
  109.2 19.7 %collective-permute-start.7 = (bf16[336,1024]{1,0:T(8,128)(2,1)S(1)}, bf16[336,1024]{1,0:T(8,128)(2,1)S(1)}, u32[]{:S(2)}, u32[]{:S(2)}) collective-permute-start(bf16[336,1024]{1,0:T(8,128)(2,1)S(1)} %get-tuple-element.42), channel_id=1, source_target_pairs={{0,1},{1,0},{2,3},{3,2},{4,5},{5,4},{6,7},{7,6},{8,9},{9,8},{10,11... | collective-permute-start | bytes 2064392 | tf_op jit(solution)/shard_map/ppermute | solution.py:70
  112.7 59.1 %collective-permute-start.10 = (bf16[528,2048]{1,0:T(8,128)(2,1)S(1)}, bf16[528,2048]{1,0:T(8,128)(2,1)S(1)}, u32[]{:S(2)}, u32[]{:S(2)}) collective-permute-start(bf16[528,2048]{1,0:T(8,128)(2,1)S(1)} %shard_map.118), channel_id=1, source_target_pairs={{0,4},{4,0},{8,12},{12,8},{16,20},{20,16},{24,28},{28,24},{32,36},... | collective-permute-start | bytes 6488072 | tf_op jit(solution)/shard_map/ppermute | solution.py:60
  117.0 54.9 %collective-permute-start.11 = (bf16[528,2048]{1,0:T(8,128)(2,1)S(1)}, bf16[528,2048]{1,0:T(8,128)(2,1)S(1)}, u32[]{:S(2)}, u32[]{:S(2)}) collective-permute-start(bf16[528,2048]{1,0:T(8,128)(2,1)S(1)} %add_convert_fusion), channel_id=1, source_target_pairs={{0,3},{1,2},{2,1},{3,0},{4,7},{5,6},{6,5},{7,4},{8,11},{9,10},{10,... | collective-permute-start | bytes 6488072 | tf_op jit(solution)/shard_map/ppermute | solution.py:65
  165.9 8.5 %collective-permute-start.9 = (bf16[128,640]{1,0:T(8,128)(2,1)S(1)}, bf16[128,640]{1,0:T(8,128)(2,1)S(1)}, u32[]{:S(2)}, u32[]{:S(2)}) collective-permute-start(bf16[128,640]{1,0:T(8,128)(2,1)S(1)} %get-tuple-element.53.pass_ref), channel_id=1, source_target_pairs={{0,3},{1,2},{2,1},{3,0},{4,7},{5,6},{6,5},{7,4},{8,11},{9,10},{10,... | collective-permute-start | bytes 491528 | tf_op jit(solution)/shard_map/ppermute | solution.py:65
  171.9 2.5 %copy-start.2 = (bf16[128,4]{0,1:T(4,128)(2,1)S(1)}, bf16[128,4]{0,1:T(4,128)(2,1)}, u32[]{:S(2)}) copy-start(bf16[128,4]{0,1:T(4,128)(2,1)} %param.10) | copy-start | bytes 3076

commit v4 on v3

--- a/solution.py
+++ b/solution.py
@@ -25,11 +25,11 @@
     )
 
 
-def local_call(body, out_shape, *operands, mib=12, **options):
+def local_call(body, out_shape, *operands, mib=12, flops=0, **options):
     return pl.pallas_call(
         body,
         out_shape=out_shape,
-        cost_estimate=pl.CostEstimate(flops=0, bytes_accessed=0, transcendentals=0),
+        cost_estimate=pl.CostEstimate(flops=flops, bytes_accessed=0, transcendentals=0),
         compiler_params=pltpu.CompilerParams(vmem_limit_bytes=mib * 1024 * 1024),
         **options,
     )(*operands)
@@ -96,10 +96,30 @@
     return jnp.where(condition, 1.0, 0.0)
 
 
-def pack_kernel(ids_ref, probs_ref, own_x_ref, own_dy_ref, got_ref, send_ref):
+def packed(wide_code, wide_weight, fold, x, dy, target, base=None):
+    wide, tokens = wide_code.shape
+    quarter = x.shape[1]
+    row = iota(wide, tokens, 0) % TILE
+    mine = row // HEAD == fold
+    head = jnp.where(mine & (wide_code == (row % HEAD).astype(f32)), 1.0, 0.0)
+    rest = mine & (wide_code == float(HEAD))
+    for side, (scale, source) in enumerate(((1.0, x), (wide_weight, dy))):
+        start = side * (quarter + LANES)
+        main = dot_f32((head * scale).astype(bf16), source, 1, 0).astype(bf16)
+        tail = jnp.zeros((wide, LANES), f32)
+        for index in range(HEAD):
+            pick = (jnp.where(rest & (row % HEAD == index), 1.0, 0.0) * scale).astype(bf16)
+            tail += dot_f32(pick, source[:, index * LANES : (index + 1) * LANES], 1, 0)
+        tail = tail.astype(bf16)
+        if base is not None:
+            main += base[:, start : start + quarter]
+            tail += base[:, start + quarter : start + quarter + LANES]
+        target[:, start : start + quarter] = main
+        target[:, start + quarter : start + quarter + LANES] = tail
+
+
+def pack_own_kernel(ids_ref, probs_ref, x_ref, dy_ref, send_ref, code_ref, weight_ref):
     ids = ids_ref[...]
-    tokens, top_count = ids.shape
-    quarter = own_x_ref.shape[1]
     wide = send_ref.shape[0]
     experts = wide // TILE
     upper = is_upper()
@@ -107,64 +127,42 @@
     probs = probs_ref[...].astype(f32)
     weight = sum(
         jnp.where(hit_of(ids, top, experts), probs[:, top : top + 1], 0.0)
-        for top in range(top_count)
+        for top in range(ids.shape[1])
     )
     spread = as_mask(iota(wide, experts, 0) // TILE == iota(wide, experts, 1)).astype(bf16)
     wide_code = dot_f32(spread, code.astype(bf16), 1, 1)
     wide_weight = dot_f32(spread, weight.astype(bf16), 1, 1)
-    row = iota(wide, tokens, 0) % TILE
-    head = wide_code == (row % HEAD).astype(f32)
-    rest = wide_code == float(HEAD)
-    edge = quarter + FOLDS * quarter // TILE
-
-    def place(first, second, scale, start):
-        main = jnp.zeros((wide, quarter), f32)
-        tail = jnp.zeros((wide, LANES), f32)
-        for fold, part in enumerate((first, second)):
-            pick = jnp.where(head & (row // HEAD == fold), scale, 0.0).astype(bf16)
-            main += dot_f32(pick, part, 1, 0)
-            for index in range(HEAD):
-                pick = jnp.where(rest & (row == fold * HEAD + index), scale, 0.0).astype(bf16)
-                tail += dot_f32(pick, part[:, index * LANES : (index + 1) * LANES], 1, 0)
-        send_ref[:, start : start + quarter] = main.astype(bf16)
-        send_ref[:, start + quarter : start + edge] = tail.astype(bf16)
-
-    own_x, own_dy = own_x_ref[...], own_dy_ref[...]
-    got_x, got_dy = got_ref[:tokens], got_ref[tokens:]
-    place(
-        jnp.where(upper, got_x, own_x),
-        jnp.where(upper, own_x, got_x),
-        jnp.ones((wide, tokens), f32),
-        0,
-    )
-    place(
-        jnp.where(upper, got_dy, own_dy), jnp.where(upper, own_dy, got_dy), wide_weight, edge
-    )
-
-
-def unpack(mine, theirs, outer, full_ref):
-    wide = mine.shape[0]
-    quarter = full_ref.shape[1] // 4
+    code_ref[...] = wide_code
+    weight_ref[...] = wide_weight
+    packed(wide_code, wide_weight, jnp.where(upper, 1, 0), x_ref[...], dy_ref[...], send_ref)
+
+
+def pack_got_kernel(code_ref, weight_ref, got_ref, base_ref, send_ref):
+    tokens = code_ref.shape[1]
+    fold = jnp.where(is_upper(), 0, 1)
+    x, dy = got_ref[:tokens], got_ref[tokens:]
+    packed(code_ref[...], weight_ref[...], fold, x, dy, send_ref, base_ref[...])
+
+
+def unpack(block, fold):
+    wide, quarter = block.shape[0], block.shape[1] - LANES
     experts = wide // TILE
     heads = experts * HEAD
     slot = iota(heads, wide, 0)
     source = iota(heads, wide, 1)
+    pick = as_mask(source == slot // HEAD * TILE + fold * HEAD + slot % HEAD).astype(bf16)
+    main = dot_f32(pick, block[:, :quarter], 1, 0)
     rest_slot = iota(experts, wide, 0)
     rest_source = iota(experts, wide, 1)
-    places = ((0, 3), (1, 2))
-    for side, columns in enumerate(places):
-        block = jnp.where(outer, mine, theirs) if side == 0 else jnp.where(outer, theirs, mine)
-        for fold, column in enumerate(columns):
-            pick = as_mask(source == slot // HEAD * TILE + fold * HEAD + slot % HEAD).astype(bf16)
-            full_ref[:heads, column * quarter : (column + 1) * quarter] = dot_f32(
-                pick, block[:, :quarter], 1, 0
-            ).astype(bf16)
-            for index in range(HEAD):
-                pick = as_mask(rest_source == rest_slot * TILE + fold * HEAD + index).astype(bf16)
-                start = column * quarter + index * LANES
-                full_ref[heads:, start : start + LANES] = dot_f32(
-                    pick, block[:, quarter:], 1, 0
-                ).astype(bf16)
+    tails = []
+    for index in range(HEAD):
+        pick = as_mask(rest_source == rest_slot * TILE + fold * HEAD + index).astype(bf16)
+        tails.append(dot_f32(pick, block[:, quarter:], 1, 0))
+    return jnp.concatenate([main, jnp.concatenate(tails, axis=1)], axis=0).astype(bf16)
+
+
+def column_block(place, quarter):
+    return pl.ds(pl.multiple_of(place * quarter, quarter), quarter)
 
 
 def load_units(sources, kind, units, target, sems):
@@ -186,7 +184,16 @@
         copy.wait()
 
 
-def back_kernel(units, mine_ref, theirs_ref, *refs):
+def own_kernel(got_ref, rows_ref, grads_ref):
+    edge = got_ref.shape[1] // 2
+    quarter = edge - LANES
+    for fold in range(FOLDS):
+        columns = slice(fold * quarter, (fold + 1) * quarter)
+        rows_ref[:, columns] = unpack(got_ref[:, :edge], fold)
+        grads_ref[:, columns] = unpack(got_ref[:, edge:], fold)
+
+
+def back_kernel(units, got_ref, own_rows, own_grads, *refs):
     sources = refs[:6]
     rows_ref, grads_ref, gate_ref, up_ref, sums_ref, given_ref = refs[6:12]
     parts = refs[12:24]
@@ -196,13 +203,22 @@
     down_copies = load_units(sources, 2, units, w_down, sems)
     outer = is_outer()
     slots = rows_ref.shape[0]
-    edge = mine_ref.shape[1] // 2
-    unpack(mine_ref[:, :edge], theirs_ref[:, :edge], outer, rows_ref)
+    quarter = rows_ref.shape[1] // 4
+    edge = quarter + LANES
+
+    def fill(target, own, block):
+        for fold, (outer_place, inner_place) in enumerate(((0, 1), (3, 2))):
+            mine = column_block(jnp.where(outer, outer_place, inner_place), quarter)
+            theirs = column_block(jnp.where(outer, inner_place, outer_place), quarter)
+            target[:, mine] = own[:, fold * quarter : (fold + 1) * quarter]
+            target[:, theirs] = unpack(block, fold)
+
+    fill(rows_ref, own_rows, got_ref[:, :edge])
     wait_all(gate_copies)
     pre_gate = dot_f32(rows_ref[...], w_gate[...], 1, 1)
     wait_all(up_copies)
     pre_up = dot_f32(rows_ref[...], w_up[...], 1, 1)
-    unpack(mine_ref[:, edge:], theirs_ref[:, edge:], outer, grads_ref)
+    fill(grads_ref, own_grads, got_ref[:, edge:])
     wait_all(down_copies)
     down_back = dot_f32(grads_ref[...], w_down[...], 1, 1)
     sigmoid = jax.nn.sigmoid(pre_gate)
@@ -235,8 +251,7 @@
 def blocks(gate_ref, up_ref, w_gate, w_up, outer, places, target, slots):
     quarter = target.shape[1] // FOLDS
     for fold, (outer_place, inner_place) in enumerate(places):
-        place = jnp.where(outer, outer_place, inner_place)
-        columns = pl.ds(pl.multiple_of(place * quarter, quarter), quarter)
+        columns = column_block(jnp.where(outer, outer_place, inner_place), quarter)
         block = dot_f32(gate_ref[...], w_gate[:, columns], 1, 0)
         block += dot_f32(up_ref[...], w_up[:, columns], 1, 0)
         target[:slots, fold * quarter : (fold + 1) * quarter] = block.astype(bf16)
@@ -254,19 +269,55 @@
     blocks(gate_ref, up_ref, w_gate, w_up, is_outer(), ((0, 1), (3, 2)), kept_ref, slots)
 
 
-def grad_kernel(units, rows_ref, grads_ref, gate_ref, up_ref, hidden_ref, part_ref):
+def grad_kernel(rows_ref, grads_ref, gate_ref, up_ref, hidden_ref, *part_refs):
+    pairs = ((gate_ref, rows_ref), (up_ref, rows_ref), (hidden_ref, grads_ref))
+    for place, (back, source) in enumerate(pairs):
+        result = dot_f32(back[...], source[...], 0, 0).astype(bf16)
+        units = result.shape[0]
+        if len(part_refs) == 1:
+            part_refs[0][place * units : (place + 1) * units] = result
+        else:
+            part_refs[place][...] = result
+
+
+def near_kernel(units, kept_ref, gate_twin, up_twin, down_twin, near_ref):
+    for place, twin in enumerate((gate_twin, up_twin, down_twin)):
+        part = slice(place * units, (place + 1) * units)
+        near_ref[part] = kept_ref[part] + twin[...]
+
+
+def total_kernel(units, near_ref, far_ref, *refs):
+    targets = refs[:3]
+    far_rows, in_sems, out_sems = refs[3:]
+    loads, stores = [], []
+    for place in range(3):
+        part = pl.ds(place * units, units)
+        copy = pltpu.make_async_copy(far_ref.at[part], far_rows.at[part], in_sems.at[place])
+        copy.start()
+        loads.append(copy)
+    for place, target in enumerate(targets):
+        part = pl.ds(place * units, units)
+        loads[place].wait()
+        far_rows[part] = near_ref[part] + far_rows[part]
+        copy = pltpu.make_async_copy(far_rows.at[part], target, out_sems.at[place])
+        copy.start()
+        stores.append(copy)
+    wait_all(stores)
+
+
+def far_kernel(
+    rows_ref, grads_ref, gate_ref, up_ref, hidden_ref, taken_ref, part_ref, taken_rows, sem
+):
+    copy = pltpu.make_async_copy(taken_ref, taken_rows, sem.at[0])
+    copy.start()
     pairs = ((gate_ref, rows_ref), (up_ref, rows_ref), (hidden_ref, grads_ref))
     for place, (back, source) in enumerate(pairs):
         result = dot_f32(back[...], source[...], 0, 0)
-        part_ref[place * units : (place + 1) * units] = result.astype(bf16)
-
-
-def total_kernel(units, kept_ref, twin_ref, far_ref, gate_ref, up_ref, down_ref):
-    for place, target in enumerate((gate_ref, up_ref, down_ref)):
+        if place == 0:
+            copy.wait()
+        units = result.shape[0]
         part = slice(place * units, (place + 1) * units)
-        target[...] = (
-            kept_ref[part].astype(f32) + twin_ref[part].astype(f32) + far_ref[part].astype(f32)
-        ).astype(bf16)
+        part_ref[part] = (result + taken_rows[part].astype(f32)).astype(bf16)
 
 
 def give_kernel(kept_ref, got_ref, give_ref):
@@ -366,15 +417,16 @@
     got_tokens, own_weights = lax.optimization_barrier((got_tokens, own_weights))
     far_weights = row_partner(own_weights)
     own_twin = other_core(own_weights)
-    send = local_call(
-        pack_kernel,
-        shape(wide, 2 * edge, bf16),
+    send_shape = shape(wide, 2 * edge, bf16)
+    base, code, weight = local_call(
+        pack_own_kernel,
+        (send_shape, shape(wide, tokens, f32), shape(wide, tokens, f32)),
         expert_ids,
         route_probs,
         activations,
         cotangent,
-        got_tokens,
-    )
+    )
+    send = local_call(pack_got_kernel, send_shape, code, weight, got_tokens, base)
     got = exchange_chips(send.reshape(experts, TILE, 2 * edge)).reshape(wide, 2 * edge)
     theirs = unit_partner(got)
     far_twin = [other_core(far_weights[i * units : (i + 1) * units]) for i in range(3)]
@@ -382,41 +434,54 @@
 
     vmem = pl.BlockSpec(memory_space=pltpu.VMEM)
     stay = pl.BlockSpec(memory_space=pl.ANY)
+    far = pl.BlockSpec(memory_space=pltpu.HBM)
     model = 4 * quarter
     unit_rows = pltpu.VMEM((4 * units, model), bf16)
     full = shape(slots, model, bf16)
     back = shape(slots, 4 * units, bf16)
     part = shape(slots, units, bf16)
+    own_half = shape(slots, 2 * quarter, bf16)
+    halves = local_call(own_kernel, (own_half,) * 2, got)
     full_rows, full_grads, gate_back, up_back, sums, given, *parts = local_call(
         functools.partial(back_kernel, units),
         (full, full, back, back)
         + (shape(EXTRA, 2 * quarter, bf16), shape(slots + EXTRA, 2 * quarter, bf16))
         + (part,) * 12,
-        got,
         theirs,
+        *halves,
         *sources,
         mib=30,
-        in_specs=[vmem] * 2 + [stay] * 6,
+        in_specs=[vmem] * 3 + [stay] * 6,
         out_specs=(vmem,) * 18,
         scratch_shapes=[unit_rows] * 3 + [pltpu.SemaphoreType.DMA((12,))],
     )
     taken = unit_partner(given)
 
-    def set_grads(place):
-        return local_call(
-            functools.partial(grad_kernel, units),
-            shape(3 * units, model, bf16),
-            full_rows,
-            full_grads,
-            *parts[3 * place : 3 * place + 3],
-            mib=16,
-        )
-
-    far_taken = other_core(set_grads(1))
-    far_grads = (set_grads(0).astype(f32) + far_taken.astype(f32)).astype(bf16)
+    def set_grads(out, *backs):
+        return local_call(grad_kernel, out, full_rows, full_grads, *backs, mib=16)
+
+    whole_part = shape(3 * units, model, bf16)
+    unit_grad = shape(units, model, bf16)
+    far_taken = other_core(set_grads(whole_part, *parts[3:6]))
+    far_grads = local_call(
+        far_kernel,
+        whole_part,
+        full_rows,
+        full_grads,
+        *parts[:3],
+        far_taken,
+        mib=16,
+        in_specs=[vmem] * 5 + [stay],
+        out_specs=vmem,
+        scratch_shapes=[
+            pltpu.VMEM((3 * units, model), bf16),
+            pltpu.SemaphoreType.DMA((1,)),
+        ],
+    )
     far_got = row_partner(far_grads)
-    near_taken = other_core(set_grads(3))
-    near_kept = set_grads(2)
+    far_grads, *near = lax.optimization_barrier((far_grads, *parts[6:]))
+    near_taken = [other_core(part) for part in set_grads((unit_grad,) * 3, *near[3:])]
+    near_kept = set_grads(whole_part, *near[:3])
     kept = local_call(
         functools.partial(keep_kernel, units),
         shape(slots + EXTRA, 2 * quarter, bf16),
@@ -433,6 +498,10 @@
 
     give = local_call(give_kernel, shape(wide, edge + LANES, bf16), kept, taken)
     back = exchange_chips(give.reshape(experts, TILE, edge + LANES)).reshape(wide, edge + LANES)
+    near_sum = local_call(
+        functools.partial(near_kernel, units), whole_part, near_kept, *near_taken
+    )
+    back, near_sum = lax.optimization_barrier((back, near_sum))
     own_sum, passed = local_call(
         combine_kernel,
         (shape(tokens, quarter, f32), shape(tokens, quarter + LANES, bf16)),
@@ -440,18 +509,19 @@
         back,
     )
     got_passed = row_partner(passed)
-    unit_grad = shape(units, model, bf16)
-    whole = pl.BlockSpec((3 * units, quarter), lambda i: (0, i))
-    third = pl.BlockSpec((units, quarter), lambda i: (0, i))
+    rows_scratch = pltpu.VMEM((3 * units, model), bf16)
     gate_grad, up_grad, down_grad = local_call(
         functools.partial(total_kernel, units),
         (unit_grad,) * 3,
-        near_kept,
-        near_taken,
+        near_sum,
         far_got,
-        grid=(4,),
-        in_specs=[whole] * 3,
-        out_specs=(third,) * 3,
+        in_specs=[vmem, far],
+        out_specs=(stay,) * 3,
+        scratch_shapes=[
+            rows_scratch,
+            pltpu.SemaphoreType.DMA((3,)),
+            pltpu.SemaphoreType.DMA((3,)),
+        ],
     )
     got_passed, gate_grad, up_grad, down_grad = lax.optimization_barrier(
         (got_passed, gate_grad, up_grad, down_grad)

time: 176 us -> 176 us (level)
  blocking collectives: 34.9 us -> 0 us
  waiting for transfers between devices: 52.9 us -> 67.8 us
  starting transfers between devices: 51.9 us -> 64.1 us
  local copies, waits for them, and re-layouts: 3.4 us -> 10.6 us
    all_to_all x1 -> x0, blocking collectives: 34.9 us -> none  [exchange_chips(): lax.all_to_all(block, 'ep', split_axis=0, concat_axis=0, axis_index_group...]
    all_to_all x1 -> x2, waiting for transfers between devices: 28.4 us -> 40.7 us  [exchange_chips(): lax.all_to_all(block, 'ep', split_axis=0, concat_axis=0, axis_index_group...]
    all_to_all x1 -> x2, starting transfers between devices: 16.5 us -> 26.1 us  [exchange_chips(): lax.all_to_all(block, 'ep', split_axis=0, concat_axis=0, axis_index_group...]
    unnamed x8 -> x40, local copies, waits for them, and re-layouts: 1.62 us -> 8.89 us
    ppermute x6 -> x8, starting transfers between devices: 12.4 us -> 16.5 us  [other_core(): return lax.ppermute(value, 'ep', pairs)]
    ppermute x2, waiting for transfers between devices: 5.86 us -> 8.29 us  [unit_partner(): return lax.ppermute(value, 'et', pairs)]
    ppermute x6 -> x8, waiting for transfers between devices: 2.14 us -> 3.64 us  [other_core(): return lax.ppermute(value, 'ep', pairs)]
    pallas_call x11 -> x14, Pallas kernels: 27.7 us -> 29.1 us  [local_call(): pl.pallas_call(body, out_shape=out_shape, cost_estimate=pl.CostEstimate(f...]
  transfers between devices with their start and end apart: 13 -> 16, of which waited for: 6 -> 10; matrix products, arithmetic and copies ran while one was open for 3% -> 3% of each run, Pallas kernels for 7% -> 9%
where the time goes in v4:
time: 176 us; the launch traced here: 175 us
  waiting for transfers between devices  67.8 us (39%)
  starting transfers between devices  64.1 us (36%)
  Pallas kernels  29.1 us (17%)
  local copies, waits for them, and re-layouts  10.6 us (6%)
  other arithmetic  2.68 us (2%)
    all_to_all x2, waiting for transfers between devices, exchange_chips(): lax.all_to_all(block, 'ep', split_axis=0, concat_axis=0, axis_index_group...  40.7 us
    pallas_call x14, Pallas kernels, local_call(): pl.pallas_call(body, out_shape=out_shape, cost_estimate=pl.CostEstimate(f...  29.1 us
    all_to_all x2, starting transfers between devices, exchange_chips(): lax.all_to_all(block, 'ep', split_axis=0, concat_axis=0, axis_index_group...  26.1 us
    ppermute x4, starting transfers between devices, row_partner(): lax.ppermute(value, 'et', [(source, count - 1 - source) for source in ran...  17 us
    ppermute x8, starting transfers between devices, other_core(): return lax.ppermute(value, 'ep', pairs)  16.5 us
    ppermute x4, waiting for transfers between devices, row_partner(): lax.ppermute(value, 'et', [(source, count - 1 - source) for source in ran...  15.2 us
    unnamed x40, local copies, waits for them, and re-layouts  8.89 us
    ppermute x2, waiting for transfers between devices, unit_partner(): return lax.ppermute(value, 'et', pairs)  8.29 us
  transfers between devices with their start and end apart: 16, of which 10 were waited for; matrix products, arithmetic and copies ran while one was open for 3% of the time, Pallas kernels for 9%

profile of v4, /device:TPU:16, one launch (start us, length us, event | category | flops | bytes accessed | tf_op | source)
XLA Modules:
  0.0 175.4 jit_solution(184562926994582651)
XLA Ops:
  1.6 4.7 %collective-permute-start = (bf16[256,512]{1,0:T(8,128)(2,1)S(1)}, bf16[256,512]{1,0:T(8,128)(2,1)S(1)}, u32[]{:S(2)}, u32[]{:S(2)}) collective-permute-start(bf16[256,512]{1,0:T(8,128)(2,1)S(1)} %pad_maximum_fusion.1), channel_id=1, source_target_pairs={{0,3},{1,2},{2,1},{3,0},{4,7},{5,6},{6,5},{7,4},{8,11},{9,10},{10,... | collective-permute-start | bytes 786440 | tf_op jit(solution)/shard_map/ppermute | solution.py:65
  11.0 1.7 pad_maximum_fusion.refs_4_
  14.7 16.5 %all-to-all-start = ((bf16[64,8,1280]{2,1,0:T(8,128)(2,1)}), bf16[64,8,1280]{2,1,0:T(8,128)(2,1)S(1)}, u32[]{:S(2)}, u32[]{:S(2)}) async-start(bf16[64,8,1280]{2,1,0:T(8,128)(2,1)} %bitcast.14), calls=%async_computation | async-start | bytes 2621440 | tf_op jit(solution)/shard_map/all_to_all | solution.py:48
  31.2 4.7 %collective-permute-start.2 = (bf16[528,2048]{1,0:T(8,128)(2,1)S(1)}, bf16[528,2048]{1,0:T(8,128)(2,1)}, u32[]{:S(2)}, u32[]{:S(2)}) collective-permute-start(bf16[528,2048]{1,0:T(8,128)(2,1)S(1)} %pad_maximum_fusion.refs_4_), channel_id=1, source_target_pairs={{0,3},{1,2},{2,1},{3,0},{4,7},{5,6},{6,5},{7,4},{8,11},{9,10},{10,... | collective-permute-start | bytes 6488072 | tf_op jit(solution)/shard_map/ppermute | solution.py:65
  35.8 1.9 %collective-permute-start.6 = (bf16[528,2048]{1,0:T(8,128)(2,1)S(1)}, bf16[528,2048]{1,0:T(8,128)(2,1)}, u32[]{:S(2)}, u32[]{:S(2)}) collective-permute-start(bf16[528,2048]{1,0:T(8,128)(2,1)S(1)} %pad_maximum_fusion.refs_4_), channel_id=1, source_target_pairs={{0,4},{4,0},{8,12},{12,8},{16,20},{20,16},{24,28},{28,24},{32,36},... | collective-permute-start | bytes 6488072 | tf_op jit(solution)/shard_map/ppermute | solution.py:60
  37.8 28.8 %all-to-all-done = bf16[64,8,1280]{2,1,0:T(8,128)(2,1)S(1)} async-done(((bf16[64,8,1280]{2,1,0:T(8,128)(2,1)}), bf16[64,8,1280]{2,1,0:T(8,128)(2,1)S(1)}, u32[]{:S(2)}, u32[]{:S(2)}) %all-to-all-start) | async-done | bytes 1310752 | tf_op jit(solution)/shard_map/all_to_all | solution.py:48
  66.5 2.3 %collective-permute-start.1 = (bf16[512,1280]{1,0:T(8,128)(2,1)S(1)}, bf16[512,1280]{1,0:T(8,128)(2,1)S(1)}, u32[]{:S(2)}, u32[]{:S(2)}) collective-permute-start(bf16[512,1280]{1,0:T(8,128)(2,1)S(1)} %bitcast.12), channel_id=1, source_target_pairs={{0,1},{1,0},{2,3},{3,2},{4,5},{5,4},{6,7},{7,6},{8,9},{9,8},{10,11... | collective-permute-start | bytes 3932168 | tf_op jit(solution)/shard_map/ppermute | solution.py:70
  68.8 13.4 %collective-permute-done.2.refs_0_ = bf16[528,2048]{1,0:T(8,128)(2,1)} collective-permute-done((bf16[528,2048]{1,0:T(8,128)(2,1)S(1)}, bf16[528,2048]{1,0:T(8,128)(2,1)}, u32[]{:S(2)}, u32[]{:S(2)}) %collective-permute-start.2) | collective-permute-done | bytes 2162720 | tf_op jit(solution)/shard_map/ppermute | solution.py:65
  82.2 1.7 fusion
  84.0 1.9 %collective-permute-start.5 = (bf16[176,2048]{1,0:T(8,128)(2,1)S(1)}, bf16[176,2048]{1,0:T(8,128)(2,1)S(1)}, u32[]{:S(2)}, u32[]{:S(2)}) collective-permute-start(bf16[176,2048]{1,0:T(8,128)(2,1)S(1)} %get-tuple-element.99), channel_id=1, source_target_pairs={{0,4},{4,0},{8,12},{12,8},{16,20},{20,16},{24,28},{28,24},{32,36},... | collective-permute-start | bytes 2162696 | tf_op jit(solution)/shard_map/ppermute | solution.py:60
  85.9 2.4 %collective-permute-start.4 = (bf16[176,2048]{1,0:T(8,128)(2,1)S(1)}, bf16[176,2048]{1,0:T(8,128)(2,1)S(1)}, u32[]{:S(2)}, u32[]{:S(2)}) collective-permute-start(bf16[176,2048]{1,0:T(8,128)(2,1)S(1)} %get-tuple-element.100), channel_id=1, source_target_pairs={{0,4},{4,0},{8,12},{12,8},{16,20},{20,16},{24,28},{28,24},{32,36},... | collective-permute-start | bytes 2162696 | tf_op jit(solution)/shard_map/ppermute | solution.py:60
  88.3 2.1 %collective-permute-start.3 = (bf16[176,2048]{1,0:T(8,128)(2,1)S(1)}, bf16[176,2048]{1,0:T(8,128)(2,1)S(1)}, u32[]{:S(2)}, u32[]{:S(2)}) collective-permute-start(bf16[176,2048]{1,0:T(8,128)(2,1)S(1)} %get-tuple-element.101), channel_id=1, source_target_pairs={{0,4},{4,0},{8,12},{12,8},{16,20},{20,16},{24,28},{28,24},{32,36},... | collective-permute-start | bytes 2162696 | tf_op jit(solution)/shard_map/ppermute | solution.py:60
  92.4 3.1 %collective-permute-done.1.got_ref = bf16[512,1280]{1,0:T(8,128)(2,1)S(1)} collective-permute-done((bf16[512,1280]{1,0:T(8,128)(2,1)S(1)}, bf16[512,1280]{1,0:T(8,128)(2,1)S(1)}, u32[]{:S(2)}, u32[]{:S(2)}) %collective-permute-start.1) | collective-permute-done | bytes 1310752 | tf_op jit(solution)/shard_map/ppermute | solution.py:70
  95.5 9.6 %shard_map.113 = (bf16[320,2048]{1,0:T(8,128)(2,1)S(1)}, bf16[320,2048]{1,0:T(8,128)(2,1)S(1)}, bf16[320,704]{1,0:T(8,128)(2,1)S(1)}, bf16[320,704]{1,0:T(8,128)...) custom-call(bf16[512,1280]{1,0:T(8,128)(2,1)S(1)} %collective-permut, ...), custom_call_target="tpu_custom_call" | custom-call | tf_op jit(solution)/shard_map/pallas_call | solution.py:29
  105.8 1.3 shard_map.116
  107.2 1.9 %collective-permute-start.8 = (bf16[528,2048]{1,0:T(8,128)(2,1)S(1)}, bf16[528,2048]{1,0:T(8,128)(2,1)S(1)}, u32[]{:S(2)}, u32[]{:S(2)}) collective-permute-start(bf16[528,2048]{1,0:T(8,128)(2,1)S(1)} %shard_map.116), channel_id=1, source_target_pairs={{0,4},{4,0},{8,12},{12,8},{16,20},{20,16},{24,28},{28,24},{32,36},... | collective-permute-start | bytes 6488072 | tf_op jit(solution)/shard_map/ppermute | solution.py:60
  109.1 2.2 %collective-permute-start.7 = (bf16[336,1024]{1,0:T(8,128)(2,1)S(1)}, bf16[336,1024]{1,0:T(8,128)(2,1)S(1)}, u32[]{:S(2)}, u32[]{:S(2)}) collective-permute-start(bf16[336,1024]{1,0:T(8,128)(2,1)S(1)} %get-tuple-element.62), channel_id=1, source_target_pairs={{0,1},{1,0},{2,3},{3,2},{4,5},{5,4},{6,7},{7,6},{8,9},{9,8},{10,11... | collective-permute-start | bytes 2064392 | tf_op jit(solution)/shard_map/ppermute | solution.py:70
  111.3 2.0 %collective-permute-done.8.taken_ref = bf16[528,2048]{1,0:T(8,128)(2,1)S(1)} collective-permute-done((bf16[528,2048]{1,0:T(8,128)(2,1)S(1)}, bf16[528,2048]{1,0:T(8,128)(2,1)S(1)}, u32[]{:S(2)}, u32[]{:S(2)}) %collective-permute-start.8) | collective-permute-done | bytes 2162720 | tf_op jit(solution)/shard_map/ppermute | solution.py:60
  113.3 3.0 %shard_map.117 = bf16[528,2048]{1,0:T(8,128)(2,1)} custom-call(bf16[320,2048]{1,0:T(8,128)(2,1)S(1)} %get-tuple-element.63.rows_ref, bf16[320,2048]{1,0:T(8,128)(2,1)S(1)} %get-tuple-element.64.grads_ref, bf16[320,176]{1,0:T(8,128)(2,1)S(1)} %get-tuple-element.65.gate_ref, bf16[320,176]{1,0:T(8,128)(2,1)S(1)} %get-tuple-element.66.up_ref, ...), custom_call_target="tpu_custom_call" | custom-call | tf_op jit(solution)/shard_map/pallas_call | solution.py:29
  116.4 3.5 %collective-permute-start.13 = (bf16[528,2048]{1,0:T(8,128)(2,1)}, bf16[528,2048]{1,0:T(8,128)(2,1)}, u32[]{:S(2)}, u32[]{:S(2)}) collective-permute-start(bf16[528,2048]{1,0:T(8,128)(2,1)} %shard_map.117), channel_id=1, source_target_pairs={{0,3},{1,2},{2,1},{3,0},{4,7},{5,6},{6,5},{7,4},{8,11},{9,10},{10,... | collective-permute-start | bytes 6488072 | tf_op jit(solution)/shard_map/ppermute | solution.py:65
  119.9 3.7 %shard_map.114.kept_ref = bf16[336,1024]{1,0:T(8,128)(2,1)S(1)} custom-call(bf16[320,704]{1,0:T(8,128)(2,1)S(1)} %get-tuple-element.59.gate_ref, bf16[320,704]{1,0:T(8,128)(2,1)S(1)} %get-tuple-element.60.up_ref, bf16[16,1024]{1,0:T(8,128)(2,1)S(1)} %get-tuple-element.61.sums_ref, bf16[528,2048]{1,0:T(8,128)(2,1)} %collective-permute-done.2.refs_0_, ...), custom_call_target="tpu_custom_call" | custom-call | tf_op jit(solution)/shard_map/pallas_call | solution.py:29
  123.6 5.2 %collective-permute-done.7.got_ref = bf16[336,1024]{1,0:T(8,128)(2,1)S(1)} collective-permute-done((bf16[336,1024]{1,0:T(8,128)(2,1)S(1)}, bf16[336,1024]{1,0:T(8,128)(2,1)S(1)}, u32[]{:S(2)}, u32[]{:S(2)}) %collective-permute-start.7) | collective-permute-done | bytes 688160 | tf_op jit(solution)/shard_map/ppermute | solution.py:70
  130.7 9.6 %all-to-all-start.1 = ((bf16[64,8,768]{2,1,0:T(8,128)(2,1)}), bf16[64,8,768]{2,1,0:T(8,128)(2,1)S(1)}, u32[]{:S(2)}, u32[]{:S(2)}) async-start(bf16[64,8,768]{2,1,0:T(8,128)(2,1)} %bitcast.16), calls=%async_computation.1 | async-start | bytes 1572864 | tf_op jit(solution)/shard_map/all_to_all | solution.py:48
  143.2 1.3 shard_map.119
  144.5 1.9 %collective-permute-start.9 = (bf16[176,2048]{1,0:T(8,128)(2,1)S(1)}, bf16[176,2048]{1,0:T(8,128)(2,1)S(1)}, u32[]{:S(2)}, u32[]{:S(2)}) collective-permute-start(bf16[176,2048]{1,0:T(8,128)(2,1)S(1)} %get-tuple-element.83), channel_id=1, source_target_pairs={{0,4},{4,0},{8,12},{12,8},{16,20},{20,16},{24,28},{28,24},{32,36},... | collective-permute-start | bytes 2162696 | tf_op jit(solution)/shard_map/ppermute | solution.py:60
  146.4 2.4 %collective-permute-start.10 = (bf16[176,2048]{1,0:T(8,128)(2,1)S(1)}, bf16[176,2048]{1,0:T(8,128)(2,1)S(1)}, u32[]{:S(2)}, u32[]{:S(2)}) collective-permute-start(bf16[176,2048]{1,0:T(8,128)(2,1)S(1)} %get-tuple-element.84), channel_id=1, source_target_pairs={{0,4},{4,0},{8,12},{12,8},{16,20},{20,16},{24,28},{28,24},{32,36},... | collective-permute-start | bytes 2162696 | tf_op jit(solution)/shard_map/ppermute | solution.py:60
  148.8 1.9 %collective-permute-start.11 = (bf16[176,2048]{1,0:T(8,128)(2,1)S(1)}, bf16[176,2048]{1,0:T(8,128)(2,1)S(1)}, u32[]{:S(2)}, u32[]{:S(2)}) collective-permute-start(bf16[176,2048]{1,0:T(8,128)(2,1)S(1)} %get-tuple-element.85), channel_id=1, source_target_pairs={{0,4},{4,0},{8,12},{12,8},{16,20},{20,16},{24,28},{28,24},{32,36},... | collective-permute-start | bytes 2162696 | tf_op jit(solution)/shard_map/ppermute | solution.py:60
  150.8 1.3 shard_map.118.kept_ref
  153.1 11.9 %all-to-all-done.1 = bf16[64,8,768]{2,1,0:T(8,128)(2,1)S(1)} async-done(((bf16[64,8,768]{2,1,0:T(8,128)(2,1)}), bf16[64,8,768]{2,1,0:T(8,128)(2,1)S(1)}, u32[]{:S(2)}, u32[]{:S(2)}) %all-to-all-start.1) | async-done | bytes 786464 | tf_op jit(solution)/shard_map/all_to_all | solution.py:48
  166.1 4.1 %collective-permute-start.12 = (bf16[128,640]{1,0:T(8,128)(2,1)S(1)}, bf16[128,640]{1,0:T(8,128)(2,1)S(1)}, u32[]{:S(2)}, u32[]{:S(2)}) collective-permute-start(bf16[128,640]{1,0:T(8,128)(2,1)S(1)} %get-tuple-element.88.pass_ref), channel_id=1, source_target_pairs={{0,3},{1,2},{2,1},{3,0},{4,7},{5,6},{6,5},{7,4},{8,11},{9,10},{10,... | collective-permute-start | bytes 491528 | tf_op jit(solution)/shard_map/ppermute | solution.py:65
  170.2 2.6 %shard_map.122 = (bf16[176,2048]{1,0:T(8,128)(2,1)}, bf16[176,2048]{1,0:T(8,128)(2,1)}, bf16[176,2048]{1,0:T(8,128)(2,1)}) custom-call(bf16[528,2048]{1,0:T(8,128)(2,1)S(1)} %shard_map.120.near_ref, bf16[528,2048]{1,0:T(8,128)(2,1)} %collective-permute-done.13.far_ref), custom_call_target="tpu_custom_call" | custom-call | tf_op jit(solution)/shard_map/pallas_call | solution.py:29
  172.8 1.7 collective-permute-done.12.got_ref
  (57 shorter events, 17.9 us)
Async XLA Ops:
  1.6 11.2 %collective-permute-start = (bf16[256,512]{1,0:T(8,128)(2,1)S(1)}, bf16[256,512]{1,0:T(8,128)(2,1)S(1)}, u32[]{:S(2)}, u32[]{:S(2)}) collective-permute-start(bf16[256,512]{1,0:T(8,128)(2,1)S(1)} %pad_maximum_fusion.1), channel_id=1, source_target_pairs={{0,3},{1,2},{2,1},{3,0},{4,7},{5,6},{6,5},{7,4},{8,11},{9,10},{10,... | collective-permute-start | bytes 786440 | tf_op jit(solution)/shard_map/ppermute | solution.py:65
  7.9 0.9 copy-start.4
  12.7 23.1 %copy-start = (bf16[528,2048]{1,0:T(8,128)(2,1)}, bf16[528,2048]{1,0:T(8,128)(2,1)S(1)}, u32[]{:S(2)}) copy-start(bf16[528,2048]{1,0:T(8,128)(2,1)S(1)} %pad_maximum_fusion.refs_4_) | copy-start | bytes 6488068
  13.6 1.1 copy-start.2
  14.7 51.9 %all-to-all-start = ((bf16[64,8,1280]{2,1,0:T(8,128)(2,1)}), bf16[64,8,1280]{2,1,0:T(8,128)(2,1)S(1)}, u32[]{:S(2)}, u32[]{:S(2)}) async-start(bf16[64,8,1280]{2,1,0:T(8,128)(2,1)} %bitcast.14), calls=%async_computation | async-start | bytes 2621440 | tf_op jit(solution)/shard_map/all_to_all | solution.py:48
  31.2 51.1 %collective-permute-start.2 = (bf16[528,2048]{1,0:T(8,128)(2,1)S(1)}, bf16[528,2048]{1,0:T(8,128)(2,1)}, u32[]{:S(2)}, u32[]{:S(2)}) collective-permute-start(bf16[528,2048]{1,0:T(8,128)(2,1)S(1)} %pad_maximum_fusion.refs_4_), channel_id=1, source_target_pairs={{0,3},{1,2},{2,1},{3,0},{4,7},{5,6},{6,5},{7,4},{8,11},{9,10},{10,... | collective-permute-start | bytes 6488072 | tf_op jit(solution)/shard_map/ppermute | solution.py:65
  35.8 55.7 %collective-permute-start.6 = (bf16[528,2048]{1,0:T(8,128)(2,1)S(1)}, bf16[528,2048]{1,0:T(8,128)(2,1)}, u32[]{:S(2)}, u32[]{:S(2)}) collective-permute-start(bf16[528,2048]{1,0:T(8,128)(2,1)S(1)} %pad_maximum_fusion.refs_4_), channel_id=1, source_target_pairs={{0,4},{4,0},{8,12},{12,8},{16,20},{20,16},{24,28},{28,24},{32,36},... | collective-permute-start | bytes 6488072 | tf_op jit(solution)/shard_map/ppermute | solution.py:60
  66.5 28.9 %copy-start.1 = (bf16[528,2048]{1,0:T(8,128)(2,1)S(1)}, bf16[528,2048]{1,0:T(8,128)(2,1)}, u32[]{:S(2)}) copy-start(bf16[528,2048]{1,0:T(8,128)(2,1)} %copy-done) | copy-start | bytes 6488068
  66.5 28.9 %collective-permute-start.1 = (bf16[512,1280]{1,0:T(8,128)(2,1)S(1)}, bf16[512,1280]{1,0:T(8,128)(2,1)S(1)}, u32[]{:S(2)}, u32[]{:S(2)}) collective-permute-start(bf16[512,1280]{1,0:T(8,128)(2,1)S(1)} %bitcast.12), channel_id=1, source_target_pairs={{0,1},{1,0},{2,3},{3,2},{4,5},{5,4},{6,7},{7,6},{8,9},{9,8},{10,11... | collective-permute-start | bytes 3932168 | tf_op jit(solution)/shard_map/ppermute | solution.py:70
  84.0 7.6 %collective-permute-start.5 = (bf16[176,2048]{1,0:T(8,128)(2,1)S(1)}, bf16[176,2048]{1,0:T(8,128)(2,1)S(1)}, u32[]{:S(2)}, u32[]{:S(2)}) collective-permute-start(bf16[176,2048]{1,0:T(8,128)(2,1)S(1)} %get-tuple-element.99), channel_id=1, source_target_pairs={{0,4},{4,0},{8,12},{12,8},{16,20},{20,16},{24,28},{28,24},{32,36},... | collective-permute-start | bytes 2162696 | tf_op jit(solution)/shard_map/ppermute | solution.py:60
  85.9 5.7 %collective-permute-start.4 = (bf16[176,2048]{1,0:T(8,128)(2,1)S(1)}, bf16[176,2048]{1,0:T(8,128)(2,1)S(1)}, u32[]{:S(2)}, u32[]{:S(2)}) collective-permute-start(bf16[176,2048]{1,0:T(8,128)(2,1)S(1)} %get-tuple-element.100), channel_id=1, source_target_pairs={{0,4},{4,0},{8,12},{12,8},{16,20},{20,16},{24,28},{28,24},{32,36},... | collective-permute-start | bytes 2162696 | tf_op jit(solution)/shard_map/ppermute | solution.py:60
  88.3 4.1 %collective-permute-start.3 = (bf16[176,2048]{1,0:T(8,128)(2,1)S(1)}, bf16[176,2048]{1,0:T(8,128)(2,1)S(1)}, u32[]{:S(2)}, u32[]{:S(2)}) collective-permute-start(bf16[176,2048]{1,0:T(8,128)(2,1)S(1)} %get-tuple-element.101), channel_id=1, source_target_pairs={{0,4},{4,0},{8,12},{12,8},{16,20},{20,16},{24,28},{28,24},{32,36},... | collective-permute-start | bytes 2162696 | tf_op jit(solution)/shard_map/ppermute | solution.py:60
  105.8 1.3 copy-start.8
  105.8 1.3 copy-start.10
  105.8 1.3 copy-start.12
  105.8 1.4 copy-start.14
  105.8 1.4 copy-start.16
  107.2 6.1 %collective-permute-start.8 = (bf16[528,2048]{1,0:T(8,128)(2,1)S(1)}, bf16[528,2048]{1,0:T(8,128)(2,1)S(1)}, u32[]{:S(2)}, u32[]{:S(2)}) collective-permute-start(bf16[528,2048]{1,0:T(8,128)(2,1)S(1)} %shard_map.116), channel_id=1, source_target_pairs={{0,4},{4,0},{8,12},{12,8},{16,20},{20,16},{24,28},{28,24},{32,36},... | collective-permute-start | bytes 6488072 | tf_op jit(solution)/shard_map/ppermute | solution.py:60
  109.1 19.7 %collective-permute-start.7 = (bf16[336,1024]{1,0:T(8,128)(2,1)S(1)}, bf16[336,1024]{1,0:T(8,128)(2,1)S(1)}, u32[]{:S(2)}, u32[]{:S(2)}) collective-permute-start(bf16[336,1024]{1,0:T(8,128)(2,1)S(1)} %get-tuple-element.62), channel_id=1, source_target_pairs={{0,1},{1,0},{2,3},{3,2},{4,5},{5,4},{6,7},{7,6},{8,9},{9,8},{10,11... | collective-permute-start | bytes 2064392 | tf_op jit(solution)/shard_map/ppermute | solution.py:70
  116.4 53.9 %collective-permute-start.13 = (bf16[528,2048]{1,0:T(8,128)(2,1)}, bf16[528,2048]{1,0:T(8,128)(2,1)}, u32[]{:S(2)}, u32[]{:S(2)}) collective-permute-start(bf16[528,2048]{1,0:T(8,128)(2,1)} %shard_map.117), channel_id=1, source_target_pairs={{0,3},{1,2},{2,1},{3,0},{4,7},{5,6},{6,5},{7,4},{8,11},{9,10},{10,... | collective-permute-start | bytes 6488072 | tf_op jit(solution)/shard_map/ppermute | solution.py:65
  130.7 34.3 %all-to-all-start.1 = ((bf16[64,8,768]{2,1,0:T(8,128)(2,1)}), bf16[64,8,768]{2,1,0:T(8,128)(2,1)S(1)}, u32[]{:S(2)}, u32[]{:S(2)}) async-start(bf16[64,8,768]{2,1,0:T(8,128)(2,1)} %bitcast.16), calls=%async_computation.1 | async-start | bytes 1572864 | tf_op jit(solution)/shard_map/all_to_all | solution.py:48
  140.3 10.4 %copy-start.7 = (bf16[320,176]{1,0:T(8,128)(2,1)S(1)}, bf16[320,176]{1,0:T(8,128)(2,1)}, u32[]{:S(2)}) copy-start(bf16[320,176]{1,0:T(8,128)(2,1)} %copy-done.6) | copy-start | bytes 337924
  140.3 10.4 %copy-start.9 = (bf16[320,176]{1,0:T(8,128)(2,1)S(1)}, bf16[320,176]{1,0:T(8,128)(2,1)}, u32[]{:S(2)}) copy-start(bf16[320,176]{1,0:T(8,128)(2,1)} %copy-done.8) | copy-start | bytes 337924
  140.4 10.4 %copy-start.11 = (bf16[320,176]{1,0:T(8,128)(2,1)S(1)}, bf16[320,176]{1,0:T(8,128)(2,1)}, u32[]{:S(2)}) copy-start(bf16[320,176]{1,0:T(8,128)(2,1)} %copy-done.10) | copy-start | bytes 337924
  140.4 1.0 copy-start.13
  141.3 0.9 copy-start.15
  142.3 0.9 copy-start.17
  144.5 7.6 %collective-permute-start.9 = (bf16[176,2048]{1,0:T(8,128)(2,1)S(1)}, bf16[176,2048]{1,0:T(8,128)(2,1)S(1)}, u32[]{:S(2)}, u32[]{:S(2)}) collective-permute-start(bf16[176,2048]{1,0:T(8,128)(2,1)S(1)} %get-tuple-element.83), channel_id=1, source_target_pairs={{0,4},{4,0},{8,12},{12,8},{16,20},{20,16},{24,28},{28,24},{32,36},... | collective-permute-start | bytes 2162696 | tf_op jit(solution)/shard_map/ppermute | solution.py:60
  146.4 5.7 %collective-permute-start.10 = (bf16[176,2048]{1,0:T(8,128)(2,1)S(1)}, bf16[176,2048]{1,0:T(8,128)(2,1)S(1)}, u32[]{:S(2)}, u32[]{:S(2)}) collective-permute-start(bf16[176,2048]{1,0:T(8,128)(2,1)S(1)} %get-tuple-element.84), channel_id=1, source_target_pairs={{0,4},{4,0},{8,12},{12,8},{16,20},{20,16},{24,28},{28,24},{32,36},... | collective-permute-start | bytes 2162696 | tf_op jit(solution)/shard_map/ppermute | solution.py:60
  148.8 4.1 %collective-permute-start.11 = (bf16[176,2048]{1,0:T(8,128)(2,1)S(1)}, bf16[176,2048]{1,0:T(8,128)(2,1)S(1)}, u32[]{:S(2)}, u32[]{:S(2)}) collective-permute-start(bf16[176,2048]{1,0:T(8,128)(2,1)S(1)} %get-tuple-element.85), channel_id=1, source_target_pairs={{0,4},{4,0},{8,12},{12,8},{16,20},{20,16},{24,28},{28,24},{32,36},... | collective-permute-start | bytes 2162696 | tf_op jit(solution)/shard_map/ppermute | solution.py:60
  166.1 8.4 %copy-start.18 = (bf16[128,4]{0,1:T(4,128)(2,1)S(1)}, bf16[128,4]{0,1:T(4,128)(2,1)}, u32[]{:S(2)}) copy-start(bf16[128,4]{0,1:T(4,128)(2,1)} %param.10) | copy-start | bytes 3076
  166.1 8.4 %collective-permute-start.12 = (bf16[128,640]{1,0:T(8,128)(2,1)S(1)}, bf16[128,640]{1,0:T(8,128)(2,1)S(1)}, u32[]{:S(2)}, u32[]{:S(2)}) collective-permute-start(bf16[128,640]{1,0:T(8,128)(2,1)S(1)} %get-tuple-element.88.pass_ref), channel_id=1, source_target_pairs={{0,3},{1,2},{2,1},{3,0},{4,7},{5,6},{6,5},{7,4},{8,11},{9,10},{10,... | collective-permute-start | bytes 491528 | tf_op jit(solution)/shard_map/ppermute | solution.py:65
  (3 other events, 2.5 us)
